TPU v7x, 256 devices: a whole 4x4x8 slice. The times are simulated.
256 devices in a mesh: pipe: 32 (over x, y, core), uly: 8 (over z).
Axes of the slice: x: 4, y: 4, z: 8, core: 2. Of those that a mesh axis runs over, the one named last changes fastest.
Arguments:
- fresh_qkv: bfloat16 [8192, 3, 3072], P(('pipe', 'uly')), may hold values from -8 to 8
- stale_cache: bfloat16 [32, 8192, 2, 3072], P('pipe', None, None, 'uly'), may hold values from -8 to 8
- plan: int32 [32], replicated, may hold values from 0 to 31, as said below
- refresh: int32 [32, 6], P('pipe'), may hold values from -1 to 31, as said below
Outputs:
- attended: bfloat16 [8192, 3072], P(('pipe', 'uly'))
Inputs may be any that keep to these rules, and one draw needn't show every extreme that they name: `plan`: a permutation of the patch ids. `refresh`: each row lists distinct ids, never the section's own patch, only patches held by sections at distance 1 to 3 along the sections, cyclically; rows hold from 0 to 6 ids, and some row holds 6.
All inputs are finite; a program needn't handle non-finite values.
Results may differ from a plain program's by a relative error of at most 0.0029.
Values may be sent and summed in bfloat16 or wider, within the bound.
No kernel may reach another device: no remote copies, remote signals or barrier semaphores. Data moves between devices by JAX's collectives and lax.ppermute only.
A program may use at most 128 MiB of HBM per device.

v0:
```python
import math

import jax
import jax.numpy as jnp
from jax import lax
from jax.sharding import PartitionSpec as P

HD = 128
SPAN = 3


def shifted(value, axis, steps):
    count = lax.axis_size(axis)
    pairs = [(source, (source + steps) % count) for source in range(count)]
    return lax.ppermute(value, axis, pairs)


def place_block(buffer, block, patch, usable):
    rows = block.shape[0]
    current = lax.dynamic_slice_in_dim(buffer, patch * rows, rows, 0)
    chosen = jnp.where(usable, block, current)
    return lax.dynamic_update_slice_in_dim(buffer, chosen, patch * rows, 0)


def shards(fresh_qkv, stale_cache, plan, refresh):
    heads = lax.all_to_all(fresh_qkv, "uly", split_axis=2, concat_axis=0, tiled=True)
    rows = heads.shape[0]
    local_width = heads.shape[2]
    sections = lax.axis_size("pipe")
    me_section = lax.axis_index("pipe")
    listed = refresh[0]
    fresh_kv = heads[:, 1:3, :]
    buffer = place_block(stale_cache[0], fresh_kv, plan[me_section], True)
    offsets = [step for step in range(1, SPAN + 1)] + [-step for step in range(1, SPAN + 1)]
    for offset in offsets:
        block = shifted(fresh_kv, "pipe", offset)
        patch = plan[(me_section - offset) % sections]
        buffer = place_block(buffer, block, patch, jnp.any(listed == patch))
    local_heads = local_width // HD
    total_rows = buffer.shape[0]
    query = heads[:, 0, :].reshape(rows, local_heads, HD)
    keys = buffer[:, 0, :].reshape(total_rows, local_heads, HD)
    values = buffer[:, 1, :].reshape(total_rows, local_heads, HD)
    factor = 1.0 / math.sqrt(HD)
    scores = jnp.einsum("qhd,khd->hqk", query, keys, preferred_element_type=jnp.float32) * factor
    top = jnp.max(scores, axis=-1, keepdims=True)
    probs = jnp.exp(scores - top)
    totals = jnp.sum(probs, axis=-1)
    weights = probs.astype(jnp.bfloat16)
    mixed = jnp.einsum("hqk,khd->qhd", weights, values, preferred_element_type=jnp.float32)
    mixed = mixed / jnp.transpose(totals)[:, :, None]
    outgoing = mixed.reshape(rows, local_width).astype(jnp.bfloat16)
    return lax.all_to_all(outgoing, "uly", split_axis=0, concat_axis=1, tiled=True)


def solution(mesh):
    placed = (P(("pipe", "uly"), None, None), P("pipe", None, None, "uly"), P(), P("pipe", None))
    return jax.shard_map(
        shards, mesh=mesh, in_specs=placed, out_specs=P(("pipe", "uly"), None), check_vma=False
    )
```

profile of v0, /device:TPU:30, one launch (start us, length us, event | category | flops | bytes accessed | tf_op | source)
XLA Modules:
  0.0 178.2 jit_solution(9901992716018393478)
XLA Ops:
  0.0 4.4 %copy.35 = bf16[32,3,3072]{0,1,2:T(4,128)(2,1)S(1)} copy(bf16[32,3,3072]{2,0,1:T(8,128)(2,1)} %param.4) | data formatting | bytes 1179648 | tf_op args[0]
  4.5 4.0 %reshape.23 = bf16[8,2,18432]{2,1,0:T(2,128)(2,1)} reshape(bf16[3072,3,32]{2,1,0:T(4,128)(2,1)S(1)} %bitcast.53) | data formatting | bytes 1179648
  8.5 8.5 %all-to-all-start = ((bf16[8,2,18432]{2,1,0:T(2,128)(2,1)}), bf16[8,2,18432]{2,1,0:T(2,128)(2,1)}, u32[]{:S(2)}, u32[]{:S(2)}) async-start(bf16[8,2,18432]{2,1,0:T(2,128)(2,1)} %reshape.23), calls=%async_computation | async-start | bytes 1179648 | tf_op jit(solution)/shard_map/all_to_all | solution.py:26
  16.9 1.6 fusion.19
  19.2 11.5 %copy.53 = bf16[1,8192,2,384]{3,1,2,0:T(8,128)(2,1)} copy(bf16[1,8192,2,384]{3,2,1,0:T(2,128)(2,1)} %param.5) | data formatting | bytes 25165824 | tf_op args[1]
  30.7 5.2 %all-to-all-done = bf16[8,2,18432]{2,1,0:T(2,128)(2,1)} async-done(((bf16[8,2,18432]{2,1,0:T(2,128)(2,1)}), bf16[8,2,18432]{2,1,0:T(2,128)(2,1)}, u32[]{:S(2)}, u32[]{:S(2)}) %all-to-all-start) | async-done | bytes 589856 | tf_op jit(solution)/shard_map/all_to_all | solution.py:26
  35.9 4.8 %reshape.24 = bf16[3072,3,32]{2,1,0:T(4,128)(2,1)S(1)} reshape(bf16[8,2,18432]{2,1,0:T(2,128)(2,1)} %all-to-all-done) | data formatting | bytes 1179648
  40.8 3.1 %copy.50 = bf16[32,3,8,384]{3,0,2,1:T(8,128)(2,1)} copy(bf16[32,3,8,384]{0,1,3,2:T(4,128)(2,1)S(1)} %bitcast.52) | data formatting | bytes 1179648 | tf_op jit(solution)/shard_map/all_to_all | solution.py:26
  43.8 1.8 %fusion.18 = (bf16[256,2,384]{2,0,1:T(8,128)(2,1)S(1)}, bf16[8192,2,384]{2,0,1:T(8,128)(2,1)}) fusion(bf16[256,3,384]{2,0,1:T(8,128)(2,1)} %bitcast.54, bf16[8192,2,384]{2,0,1:T(8,128)(2,1)} %bitcast.49, s32[]{:T(128)S(6)} %select_n.119), kind=kLoop, calls=%fused_computation.27 | loop fusion | bytes 1179652 | tf_op jit(solution)/shard_map/slice | solution.py:32
  49.6 4.5 %compare_reduce_fusion = (pred[]{:T(512)}, pred[]{:T(512)}, pred[]{:T(512)}, pred[]{:T(512)}, pred[]{:T(512)}, /*index=5*/pred[]{:T(512)}) fusion(s32[1,6]{1,0:T(1,128)S(1)} %copy-done, s32[]{:T(128)} %bitcast.11, s32[]{:T(128)} %bitcast.9, s32[]{:T(128)} %bitcast.8, s32[]{:T(128)} %bitcast.7, s32[]{:T(128)} %bitcast.6, s32[]{:T(128)} %bitcast.10), kind=kLoop, calls=%fused_computation.19 | loop fusion | flops 66 | bytes 54 | tf_op jit(solution)/shard_map/reduce_or | solution.py:38
  54.0 0.9 slice.19
  55.0 2.0 %collective-permute-start.4 = (bf16[256,2,384]{2,0,1:T(8,128)(2,1)S(1)}, bf16[256,2,384]{2,0,1:T(8,128)(2,1)S(1)}, u32[]{:S(2)}, u32[]{:S(2)}) collective-permute-start(bf16[256,2,384]{2,0,1:T(8,128)(2,1)S(1)} %get-tuple-element.13), channel_id=1, source_target_pairs={{0,240},{8,248},{16,0},{24,8},{32,16},{40,24},{48,32},{56,40},{64,... | collective-permute-start | bytes 1179656 | tf_op jit(solution)/shard_map/ppermute | solution.py:15
  57.0 1.2 collective-permute-start.3
  58.1 3.0 %collective-permute-start.2 = (bf16[256,2,384]{2,0,1:T(8,128)(2,1)S(1)}, bf16[256,2,384]{2,0,1:T(8,128)(2,1)S(1)}, u32[]{:S(2)}, u32[]{:S(2)}) collective-permute-start(bf16[256,2,384]{2,0,1:T(8,128)(2,1)S(1)} %get-tuple-element.13), channel_id=1, source_target_pairs={{0,24},{8,32},{16,40},{24,48},{32,56},{40,64},{48,72},{56,80},{64,... | collective-permute-start | bytes 1179656 | tf_op jit(solution)/shard_map/ppermute | solution.py:15
  61.2 0.5 collective-permute-start.5
  61.8 2.5 %select_dynamic-update-slice_fusion.5 = bf16[8192,2,384]{2,0,1:T(8,128)(2,1)} fusion(bf16[8192,2,384]{2,0,1:T(8,128)(2,1)} %get-tuple-element.14, s32[]{:T(128)S(6)} %select_n.123, bf16[256,2,384]{2,0,1:T(8,128)(2,1)S(1)} %collective-permute-done, pred[]{:T(512)} %get-tuple-element.9), kind=kLoop, calls=%fused_computation.17 | loop fusion | flops 196608 | bytes 1180164 | tf_op jit(solution)/shard_map/dynamic_update_slice | solution.py:22
  64.3 2.4 %select_dynamic-update-slice_fusion.4 = bf16[8192,2,384]{2,0,1:T(8,128)(2,1)} fusion(bf16[8192,2,384]{2,0,1:T(8,128)(2,1)} %select_dynamic-update-slice_fusion.5, s32[]{:T(128)S(6)} %select_n.128, bf16[256,2,384]{2,0,1:T(8,128)(2,1)S(1)} %collective-permute-done.1, pred[]{:T(512)} %get-tuple-element.8), kind=kLoop, calls=%fused_computation.16 | loop fusion | flops 196608 | bytes 1180164 | tf_op jit(solution)/shard_map/dynamic_update_slice | solution.py:22
  66.7 20.5 %collective-permute-done.2 = bf16[256,2,384]{2,0,1:T(8,128)(2,1)S(1)} collective-permute-done((bf16[256,2,384]{2,0,1:T(8,128)(2,1)S(1)}, bf16[256,2,384]{2,0,1:T(8,128)(2,1)S(1)}, u32[]{:S(2)}, u32[]{:S(2)}) %collective-permute-start.2) | collective-permute-done | bytes 393248 | tf_op jit(solution)/shard_map/ppermute | solution.py:15
  87.2 2.5 %select_dynamic-update-slice_fusion.3 = bf16[8192,2,384]{2,0,1:T(8,128)(2,1)} fusion(bf16[8192,2,384]{2,0,1:T(8,128)(2,1)} %select_dynamic-update-slice_fusion.4, s32[]{:T(128)S(6)} %select_n.133, bf16[256,2,384]{2,0,1:T(8,128)(2,1)S(1)} %collective-permute-done.2, pred[]{:T(512)} %get-tuple-element.7), kind=kLoop, calls=%fused_computation.15 | loop fusion | flops 196608 | bytes 1180164 | tf_op jit(solution)/shard_map/dynamic_update_slice | solution.py:22
  89.7 2.5 %select_dynamic-update-slice_fusion.2 = bf16[8192,2,384]{2,0,1:T(8,128)(2,1)} fusion(bf16[8192,2,384]{2,0,1:T(8,128)(2,1)} %select_dynamic-update-slice_fusion.3, s32[]{:T(128)S(6)} %select_n.138, bf16[256,2,384]{2,0,1:T(8,128)(2,1)S(1)} %collective-permute-done.3, pred[]{:T(512)} %get-tuple-element.6), kind=kLoop, calls=%fused_computation.14 | loop fusion | flops 196608 | bytes 1180164 | tf_op jit(solution)/shard_map/dynamic_update_slice | solution.py:22
  92.2 2.5 %select_dynamic-update-slice_fusion.1 = bf16[8192,2,384]{2,0,1:T(8,128)(2,1)} fusion(bf16[8192,2,384]{2,0,1:T(8,128)(2,1)} %select_dynamic-update-slice_fusion.2, s32[]{:T(128)S(6)} %select_n.143, bf16[256,2,384]{2,0,1:T(8,128)(2,1)S(1)} %collective-permute-done.4, pred[]{:T(512)} %get-tuple-element.10), kind=kLoop, calls=%fused_computation.13 | loop fusion | flops 196608 | bytes 1180164 | tf_op jit(solution)/shard_map/dynamic_update_slice | solution.py:22
  94.7 2.5 %select_dynamic-update-slice_fusion = bf16[8192,2,384]{2,0,1:T(8,128)(2,1)} fusion(bf16[8192,2,384]{2,0,1:T(8,128)(2,1)} %select_dynamic-update-slice_fusion.1, s32[]{:T(128)S(6)} %select_n.148, bf16[256,2,384]{2,0,1:T(8,128)(2,1)S(1)} %collective-permute-done.5, pred[]{:T(512)} %get-tuple-element.5), kind=kLoop, calls=%fused_computation.12 | loop fusion | flops 196608 | bytes 1180164 | tf_op jit(solution)/shard_map/dynamic_update_slice | solution.py:22
  97.2 10.2 %fusion.17 = (bf16[8192,1,384]{2,0,1:T(8,128)(2,1)}, bf16[8192,1,384]{2,0,1:T(8,128)(2,1)}) fusion(bf16[8192,2,384]{2,0,1:T(8,128)(2,1)} %select_dynamic-update-slice_fusion), kind=kLoop, calls=%fused_computation.26 | loop fusion | bytes 25165824 | tf_op jit(solution)/shard_map/slice | solution.py:42
  107.5 8.6 %copy.39 = bf16[8192,1,384]{0,2,1:T(8,128)(2,1)} copy(bf16[8192,1,384]{2,0,1:T(8,128)(2,1)} %get-tuple-element.11) | data formatting | bytes 12582912 | tf_op jit(solution)/shard_map/slice | solution.py:42
  116.0 8.5 %copy.38 = bf16[8192,1,384]{0,2,1:T(8,128)(2,1)} copy(bf16[8192,1,384]{2,0,1:T(8,128)(2,1)} %get-tuple-element.12) | data formatting | bytes 12582912 | tf_op jit(solution)/shard_map/slice | solution.py:43
  124.6 14.6 %bitcast_reduce_fusion = (f32[3,256]{1,0:T(4,128)S(1)}, f32[3,8192,256]{2,1,0:T(8,128)}) fusion(bf16[8192,3,128]{0,2,1:T(8,128)(2,1)} %bitcast.50, bf16[256,3,128]{0,2,1:T(8,128)(2,1)S(1)} %bitcast.56), kind=kOutput, calls=%fused_computation.1 | convolution fusion | flops 1623194880 | bytes 31656960 | tf_op jit(solution)/shard_map/qhd,khd->hqk/dot_general | solution.py:45
  139.1 11.6 %fusion.1 = f32[3,256]{1,0:T(4,128)S(1)} fusion(f32[3,8192,256]{2,1,0:T(8,128)} %get-tuple-element.23, f32[3,256]{1,0:T(4,128)S(1)} %get-tuple-element.22), kind=kLoop, calls=%fused_computation.3 | loop fusion | flops 18873600 | bytes 25171968 | tf_op jit(solution)/shard_map/reduce_sum | solution.py:48
  150.7 14.2 %fusion.13 = bf16[256,3,128]{0,2,1:T(8,128)(2,1)S(1)} fusion(bf16[8192,3,128]{0,2,1:T(8,128)(2,1)} %bitcast.51, f32[3,8192,256]{2,1,0:T(8,128)} %get-tuple-element.23, f32[3,256]{1,0:T(4,128)S(1)} %get-tuple-element.22, f32[256,3]{0,1:T(4,128)S(1)} %bitcast.58), kind=kOutput, calls=%fused_computation.11 | convolution fusion | flops 1629683712 | bytes 31660032 | tf_op jit(solution)/shard_map/hqk,khd->qhd/dot_general | solution.py:50
  164.9 0.2 copy.44
  165.1 0.2 convert_element_type.12
  165.3 12.2 %all_to_all.34 = bf16[8,32,384]{2,1,0:T(8,128)(2,1)S(1)} all-to-all(bf16[8,32,384]{2,1,0:T(8,128)(2,1)S(1)} %convert_element_type.12), channel_id=1, replica_groups=mesh['pipe'=32,'uly'=8] {'uly'}, dimensions={0} | all-to-all | bytes 393216 | tf_op jit(solution)/shard_map/all_to_all | solution.py:53
  177.5 0.7 copy.51
  (10 shorter events, 0.3 us)
Async XLA Ops:
  8.5 27.5 %all-to-all-start = ((bf16[8,2,18432]{2,1,0:T(2,128)(2,1)}), bf16[8,2,18432]{2,1,0:T(2,128)(2,1)}, u32[]{:S(2)}, u32[]{:S(2)}) async-start(bf16[8,2,18432]{2,1,0:T(2,128)(2,1)} %reshape.23), calls=%async_computation | async-start | bytes 1179648 | tf_op jit(solution)/shard_map/all_to_all | solution.py:26
  19.2 30.3 %copy-start = (s32[1,6]{1,0:T(1,128)S(1)}, s32[1,6]{1,0:T(1,128)}, u32[]{:S(2)}) copy-start(s32[1,6]{1,0:T(1,128)} %param.7) | copy-start | bytes 76
  45.6 15.6 %collective-permute-start = (bf16[256,2,384]{2,0,1:T(8,128)(2,1)S(1)}, bf16[256,2,384]{2,0,1:T(8,128)(2,1)S(1)}, u32[]{:S(2)}, u32[]{:S(2)}) collective-permute-start(bf16[256,2,384]{2,0,1:T(8,128)(2,1)S(1)} %get-tuple-element.13), channel_id=1, source_target_pairs={{0,8},{8,16},{16,24},{24,32},{32,40},{40,48},{48,56},{56,64},{64,7... | collective-permute-start | bytes 1179656 | tf_op jit(solution)/shard_map/ppermute | solution.py:15
  45.6 18.6 %collective-permute-start.1 = (bf16[256,2,384]{2,0,1:T(8,128)(2,1)S(1)}, bf16[256,2,384]{2,0,1:T(8,128)(2,1)S(1)}, u32[]{:S(2)}, u32[]{:S(2)}) collective-permute-start(bf16[256,2,384]{2,0,1:T(8,128)(2,1)S(1)} %get-tuple-element.13), channel_id=1, source_target_pairs={{0,16},{8,24},{16,32},{24,40},{32,48},{40,56},{48,64},{56,72},{64,... | collective-permute-start | bytes 1179656 | tf_op jit(solution)/shard_map/ppermute | solution.py:15
  55.0 37.2 %collective-permute-start.4 = (bf16[256,2,384]{2,0,1:T(8,128)(2,1)S(1)}, bf16[256,2,384]{2,0,1:T(8,128)(2,1)S(1)}, u32[]{:S(2)}, u32[]{:S(2)}) collective-permute-start(bf16[256,2,384]{2,0,1:T(8,128)(2,1)S(1)} %get-tuple-element.13), channel_id=1, source_target_pairs={{0,240},{8,248},{16,0},{24,8},{32,16},{40,24},{48,32},{56,40},{64,... | collective-permute-start | bytes 1179656 | tf_op jit(solution)/shard_map/ppermute | solution.py:15
  57.0 32.8 %collective-permute-start.3 = (bf16[256,2,384]{2,0,1:T(8,128)(2,1)S(1)}, bf16[256,2,384]{2,0,1:T(8,128)(2,1)S(1)}, u32[]{:S(2)}, u32[]{:S(2)}) collective-permute-start(bf16[256,2,384]{2,0,1:T(8,128)(2,1)S(1)} %get-tuple-element.13), channel_id=1, source_target_pairs={{0,248},{8,0},{16,8},{24,16},{32,24},{40,32},{48,40},{56,48},{64,5... | collective-permute-start | bytes 1179656 | tf_op jit(solution)/shard_map/ppermute | solution.py:15
  58.1 29.1 %collective-permute-start.2 = (bf16[256,2,384]{2,0,1:T(8,128)(2,1)S(1)}, bf16[256,2,384]{2,0,1:T(8,128)(2,1)S(1)}, u32[]{:S(2)}, u32[]{:S(2)}) collective-permute-start(bf16[256,2,384]{2,0,1:T(8,128)(2,1)S(1)} %get-tuple-element.13), channel_id=1, source_target_pairs={{0,24},{8,32},{16,40},{24,48},{32,56},{40,64},{48,72},{56,80},{64,... | collective-permute-start | bytes 1179656 | tf_op jit(solution)/shard_map/ppermute | solution.py:15
  61.2 33.4 %collective-permute-start.5 = (bf16[256,2,384]{2,0,1:T(8,128)(2,1)S(1)}, bf16[256,2,384]{2,0,1:T(8,128)(2,1)S(1)}, u32[]{:S(2)}, u32[]{:S(2)}) collective-permute-start(bf16[256,2,384]{2,0,1:T(8,128)(2,1)S(1)} %get-tuple-element.13), channel_id=1, source_target_pairs={{0,232},{8,240},{16,248},{24,0},{32,8},{40,16},{48,24},{56,32},{64... | collective-permute-start | bytes 1179656 | tf_op jit(solution)/shard_map/ppermute | solution.py:15
where the time goes:
time: 180 us; the launch traced here: 178 us
  local copies, waits for them, and re-layouts  60.7 us (34%)
  other arithmetic  30.9 us (17%)
  matrix products  28.8 us (16%)
  waiting for transfers between devices  25.8 us (14%)
  starting transfers between devices  15.3 us (8%)
  blocking collectives  12.2 us (7%)
  between operations  4.53 us (3%)
    unnamed x6, local copies, waits for them, and re-layouts  24.8 us
    ppermute x6, waiting for transfers between devices, shifted(): return lax.ppermute(value, axis, pairs)  20.6 us
    slice x2, local copies, waits for them, and re-layouts, shards(): keys = buffer[:, 0, :].reshape(total_rows, local_heads, HD)  18.8 us
    dynamic_update_slice x6, other arithmetic, place_block(): return lax.dynamic_update_slice_in_dim(buffer, chosen, patch * rows, 0)  14.9 us
    dot_general x1, matrix products, shards(): jnp.einsum('qhd,khd->hqk', query, keys, preferred_element_type=jnp.float32)  14.6 us
    dot_general x1, matrix products, shards(): jnp.einsum('hqk,khd->qhd', weights, values, preferred_element_type=jnp.fl...  14.2 us
    all_to_all x1, blocking collectives, shards(): lax.all_to_all(outgoing, 'uly', split_axis=0, concat_axis=1, tiled=True)  12.2 us
    reduce_sum x1, other arithmetic, shards(): totals = jnp.sum(probs, axis=-1)  11.6 us
  transfers between devices with their start and end apart: 7, of which 2 were waited for; matrix products, arithmetic and copies ran while one was open for 17% of the time, Pallas kernels for 0%

commit v1 on v0

v1 whole, which is shorter than its diff:
```python
import functools
import math

import jax
import jax.numpy as jnp
from jax import lax
from jax.experimental import pallas as pl
from jax.experimental.pallas import tpu as pltpu
from jax.sharding import PartitionSpec as P

HD = 128
PT = 256
LOCAL = 3
WIDE = LOCAL * HD
PATCHES = 32
SLOTS = 6
SCALE = math.log2(math.e) / math.sqrt(HD)
GROUP = 4
HALF = 16
VMEM_BYTES = 50 * 1024 * 1024


def scores_of(query, keys):
    return lax.dot_general(query, keys, (((1,), (1,)), ((), ())), preferred_element_type=jnp.float32)


def absorb(head, scores, values, top_ref, sum_ref, acc_ref):
    before = top_ref[head]
    top = jnp.maximum(before, jnp.max(scores, axis=1, keepdims=True) * SCALE)
    fade = jnp.exp2(before - top)
    total = sum_ref[head] * fade
    parts = []
    for start in range(0, values.shape[0], HD):
        probs = jnp.exp2(scores[:, start:start + HD] * SCALE - top)
        total = total + probs
        parts.append(probs.astype(jnp.bfloat16))
    weights = jnp.concatenate(parts, axis=1)
    mixed = jnp.dot(weights, values, preferred_element_type=jnp.float32)
    acc_ref[head] = acc_ref[head] * fade + mixed
    sum_ref[head] = total
    top_ref[head] = top


def attend(query_of, keys_of, values_of, state):
    scores = [scores_of(query_of(head), keys_of(head)) for head in range(LOCAL)]
    for head in range(LOCAL):
        absorb(head, scores[head], values_of(head), *state)


def columns(head):
    return slice(head * HD, (head + 1) * HD)


def stale_kernel(least, most, me_ref, plan_ref, refresh_ref, query_ref, cache_ref, *rest):
    taken, state, (held, arrived) = rest[:-5], rest[-5:-2], rest[-2:]
    own = plan_ref[me_ref[0]]
    count = jnp.int32(0)
    for patch in range(PATCHES):
        fresh = own == patch
        for slot in range(SLOTS):
            fresh = jnp.logical_or(fresh, refresh_ref[0, slot] == patch)
        wanted = jnp.logical_not(fresh) & (count >= least) & (count < most)

        @pl.when(wanted)
        def _(patch=patch, place=count - least):
            pltpu.make_async_copy(
                cache_ref.at[:, pl.ds(patch * PT, PT), :], held.at[:, place], arrived.at[place]
            ).start()

        count = count + jnp.where(fresh, 0, 1)
    count = jnp.minimum(count, most) - least
    if taken:
        for source, target in zip(taken, state):
            target[...] = source[...]
    else:
        for target, value in zip(state, (-jnp.inf, 0.0, 0.0)):
            target[...] = jnp.full(target.shape, value, jnp.float32)

    def step(first, width):
        for slot in range(width):
            pltpu.make_async_copy(
                cache_ref.at[:, pl.ds(0, PT), :], held.at[:, first + slot], arrived.at[first + slot]
            ).wait()
        attend(
            lambda head: query_ref[:, :, columns(head)].reshape(PT, HD),
            lambda head: held[0, pl.ds(first, width), :, columns(head)].reshape(width * PT, HD),
            lambda head: held[1, pl.ds(first, width), :, columns(head)].reshape(width * PT, HD),
            state,
        )

    groups = count // GROUP

    @pl.loop(0, groups)
    def _(group):
        step(group * GROUP, GROUP)

    @pl.loop(groups * GROUP, count)
    def _(slot):
        step(slot, 1)


def stale_attention(least, most, me, plan, refresh, query, cache, taken=()):
    state = jax.ShapeDtypeStruct((LOCAL, PT, HD), jnp.float32)
    smem = pl.BlockSpec(memory_space=pltpu.SMEM)
    vmem = pl.BlockSpec(memory_space=pltpu.VMEM)
    keys = (most - least) * PT
    return pl.pallas_call(
        functools.partial(stale_kernel, least, most),
        out_shape=(state, state, state),
        in_specs=[smem, smem, smem, vmem, pl.BlockSpec(memory_space=pl.ANY)] + [vmem] * len(taken),
        out_specs=(vmem, vmem, vmem),
        scratch_shapes=[
            pltpu.VMEM((2, most - least, PT, WIDE), jnp.bfloat16),
            pltpu.SemaphoreType.DMA((most - least,)),
        ],
        compiler_params=pltpu.CompilerParams(vmem_limit_bytes=VMEM_BYTES),
        cost_estimate=pl.CostEstimate(
            flops=8 * LOCAL * PT * keys * HD, bytes_accessed=2 * keys * WIDE * 2, transcendentals=LOCAL * PT * keys
        ),
        name="stale_attention",
    )(me, plan, refresh, query, cache, *taken)


def fresh_kernel(me_ref, plan_ref, refresh_ref, query_ref, top_in, sum_in, acc_in, *rest):
    blocks, (out_ref, top_ref, sum_ref, acc_ref) = rest[:7], rest[7:]
    top_ref[...] = top_in[...]
    sum_ref[...] = sum_in[...]
    acc_ref[...] = acc_in[...]
    me = me_ref[0]

    def step(block):
        attend(
            lambda head: query_ref[:, :, columns(head)].reshape(PT, HD),
            lambda head: block[:, 0, :, columns(head)].reshape(PT, HD),
            lambda head: block[:, 1, :, columns(head)].reshape(PT, HD),
            (top_ref, sum_ref, acc_ref),
        )

    step(blocks[0])
    sections = PATCHES
    even = me % 2 == 0
    sign = jnp.where(even, 1, -1)
    origins = (me - 2, me + 2, me - 3 * sign, me + sign, me + sign - 2, me + sign + 2)
    for origin, block in zip(origins, blocks[1:]):
        patch = plan_ref[(origin + sections) % sections]
        listed = refresh_ref[0, 0] == patch
        for slot in range(1, SLOTS):
            listed = jnp.logical_or(listed, refresh_ref[0, slot] == patch)

        @pl.when(listed)
        def _(block=block):
            step(block)

    for head in range(LOCAL):
        total = jnp.sum(sum_ref[head], axis=1, keepdims=True)
        done = (acc_ref[head] / total).astype(jnp.bfloat16)
        out_ref[:, :, head * HD:(head + 1) * HD] = done.reshape(out_ref.shape[0], out_ref.shape[1], HD)


def fresh_attention(me, plan, refresh, query, state, blocks):
    smem = pl.BlockSpec(memory_space=pltpu.SMEM)
    vmem = pl.BlockSpec(memory_space=pltpu.VMEM)
    held = pltpu.VMEM((LOCAL, PT, HD), jnp.float32)
    return pl.pallas_call(
        fresh_kernel,
        out_shape=jax.ShapeDtypeStruct(query.shape, jnp.bfloat16),
        in_specs=[smem] * 3 + [vmem] * 11,
        out_specs=vmem,
        scratch_shapes=[held, held, held],
        compiler_params=pltpu.CompilerParams(vmem_limit_bytes=32 * 1024 * 1024),
        name="fresh_attention",
    )(me, plan, refresh, query, *state, *blocks)


def move(value, target):
    count = lax.axis_size("pipe")
    return lax.ppermute(value, "pipe", [(source, target(source) % count) for source in range(count)])


def exchange(value):
    return lax.all_to_all(value, "uly", split_axis=0, concat_axis=0, tiled=True)


def shards(fresh_qkv, stale_cache, plan, refresh):
    rows = fresh_qkv.shape[0]
    devices = lax.axis_size("uly")
    me = lax.axis_index("pipe").astype(jnp.int32).reshape(1)
    outgoing = fresh_qkv.reshape(rows, 3, devices, WIDE).transpose(2, 1, 0, 3)
    heads = exchange(outgoing)
    cache = stale_cache[0].transpose(1, 0, 2)
    heads, cache = lax.optimization_barrier((heads, cache))
    own, query = heads[:, 1:3], heads[:, 0]
    behind = move(own, lambda s: s + 2)
    ahead = move(own, lambda s: s - 2)
    far = move(own, lambda s: s + 3 if s % 2 else s - 3)
    twin = lambda s: s ^ 1
    beside = move(own, twin)
    state = stale_attention(0, HALF, me, plan, refresh, query, cache)
    state, behind, ahead = lax.optimization_barrier((state, behind, ahead))
    beside_behind = move(behind, twin)
    beside_ahead = move(ahead, twin)
    state = stale_attention(HALF, PATCHES - 1, me, plan, refresh, query, cache, state)
    blocks = (own, behind, ahead, far, beside, beside_behind, beside_ahead)
    mixed = fresh_attention(me, plan, refresh, query, state, blocks)
    back = exchange(mixed)
    return back.transpose(1, 0, 2).reshape(rows, devices * WIDE)


def solution(mesh):
    placed = (P(("pipe", "uly"), None, None), P("pipe", None, None, "uly"), P(), P("pipe", None))
    return jax.shard_map(
        shards, mesh=mesh, in_specs=placed, out_specs=P(("pipe", "uly"), None), check_vma=False
    )
```

time: 180 us -> 75.6 us (0.42)
  the two profiles are of different devices: /device:TPU:30 before, /device:TPU:26 now
where the time goes in v1:
time: 75.6 us; the launch traced here: 75 us
  Pallas kernels  16.5 us (22%)
  waiting for transfers between devices  16.4 us (22%)
  local copies, waits for them, and re-layouts  14.3 us (19%)
  blocking collectives  14.3 us (19%)
  starting transfers between devices  13.4 us (18%)
    all_to_all x1, blocking collectives, exchange(): return lax.all_to_all(value, 'uly', split_axis=0, concat_axis=0, tiled=True)  14.3 us
    pallas_call x2, Pallas kernels, stale_attention(): pl.pallas_call(functools.partial(stale_kernel, least, most), out_shape=(s...  13.5 us
    unnamed x5, local copies, waits for them, and re-layouts  11.5 us
    ppermute x6, waiting for transfers between devices, move(): lax.ppermute(value, 'pipe', [(source, target(source) % count) for source...  9.03 us
    all_to_all x1, starting transfers between devices, exchange(): return lax.all_to_all(value, 'uly', split_axis=0, concat_axis=0, tiled=True)  8.47 us
    all_to_all x1, waiting for transfers between devices, exchange(): return lax.all_to_all(value, 'uly', split_axis=0, concat_axis=0, tiled=True)  7.36 us
    ppermute x6, starting transfers between devices, move(): lax.ppermute(value, 'pipe', [(source, target(source) % count) for source...  4.98 us
    pallas_call x1, Pallas kernels, fresh_attention(): pl.pallas_call(fresh_kernel, out_shape=jax.ShapeDtypeStruct(query.shape,...  3.06 us
  transfers between devices with their start and end apart: 7, of which 3 were waited for; matrix products, arithmetic and copies ran while one was open for 15% of the time, Pallas kernels for 18%

profile of v1, /device:TPU:26, one launch (start us, length us, event | category | flops | bytes accessed | tf_op | source)
XLA Modules:
  0.0 75.0 jit_solution(16933327635671368704)
XLA Ops:
  0.0 2.0 %copy.14 = bf16[3,4,8,8,384]{4,3,1,0,2:T(8,128)(2,1)} copy(bf16[3,4,8,8,384]{4,3,2,1,0:T(8,128)(2,1)} %bitcast.21) | data formatting | bytes 1179648 | tf_op jit(solution)/shard_map/reshape | solution.py:188
  2.0 8.5 %all-to-all-start = ((bf16[8,3,32,384]{3,2,1,0:T(8,128)(2,1)}), bf16[8,3,32,384]{3,2,1,0:T(8,128)(2,1)S(1)}, u32[]{:S(2)}, u32[]{:S(2)}) async-start(bf16[8,3,32,384]{3,2,1,0:T(8,128)(2,1)} %bitcast.17), calls=%async_computation | async-start | bytes 1179648 | tf_op jit(solution)/shard_map/all_to_all | solution.py:181
  10.4 0.0 copy-start
  10.4 0.0 copy-start.1
  10.5 11.5 %copy.13 = bf16[1,8192,2,384]{3,1,2,0:T(8,128)(2,1)} copy(bf16[1,8192,2,384]{3,2,1,0:T(2,128)(2,1)} %param.5) | data formatting | bytes 25165824 | tf_op args[1]
  22.0 7.4 %all-to-all-done = bf16[8,3,32,384]{3,2,1,0:T(8,128)(2,1)S(1)} async-done(((bf16[8,3,32,384]{3,2,1,0:T(8,128)(2,1)}), bf16[8,3,32,384]{3,2,1,0:T(8,128)(2,1)S(1)}, u32[]{:S(2)}, u32[]{:S(2)}) %all-to-all-start) | async-done | bytes 589856 | tf_op jit(solution)/shard_map/all_to_all | solution.py:181
  29.4 1.2 %collective-permute-start = (bf16[8,2,32,384]{3,2,1,0:T(8,128)(2,1)S(1)}, bf16[8,2,32,384]{3,2,1,0:T(8,128)(2,1)S(1)}, u32[]{:S(2)}, u32[]{:S(2)}) collective-permute-start(bf16[8,2,32,384]{3,2,1,0:T(8,128)(2,1)S(1)} %slice.7.rest_0_), channel_id=1, source_target_pairs={{0,16},{8,24},{16,32},{24,40},{32,48},{40,56},{48,64},{56,72},{64,... | collective-permute-start | bytes 1179656 | tf_op jit(solution)/shard_map/ppermute | solution.py:177
  30.6 0.9 %collective-permute-start.1 = (bf16[8,2,32,384]{3,2,1,0:T(8,128)(2,1)S(1)}, bf16[8,2,32,384]{3,2,1,0:T(8,128)(2,1)S(1)}, u32[]{:S(2)}, u32[]{:S(2)}) collective-permute-start(bf16[8,2,32,384]{3,2,1,0:T(8,128)(2,1)S(1)} %slice.7.rest_0_), channel_id=1, source_target_pairs={{0,240},{8,248},{16,0},{24,8},{32,16},{40,24},{48,32},{56,40},{64,... | collective-permute-start | bytes 1179656 | tf_op jit(solution)/shard_map/ppermute | solution.py:177
  31.5 0.4 collective-permute-start.2
  31.9 2.0 %collective-permute-start.3 = (bf16[8,2,32,384]{3,2,1,0:T(8,128)(2,1)S(1)}, bf16[8,2,32,384]{3,2,1,0:T(8,128)(2,1)S(1)}, u32[]{:S(2)}, u32[]{:S(2)}) collective-permute-start(bf16[8,2,32,384]{3,2,1,0:T(8,128)(2,1)S(1)} %slice.7.rest_0_), channel_id=1, source_target_pairs={{0,8},{8,0},{16,24},{24,16},{32,40},{40,32},{48,56},{56,48},{64,72... | collective-permute-start | bytes 1179656 | tf_op jit(solution)/shard_map/ppermute | solution.py:177
  33.9 0.0 copy-done
  33.9 0.0 copy-done.1
  33.9 7.4 %stale_attention.2 = (f32[3,256,128]{2,1,0:T(8,128)S(1)}, f32[3,256,128]{2,1,0:T(8,128)S(1)}, f32[3,256,128]{2,1,0:T(8,128)S(1)}) custom-call(s32[1]{0:T(128)} %bitcast.me_ref, s32[32]{0:T(128)S(1)} %copy-done, s32[1,6]{1,0:T(1,128)S(1)} %copy-done.1, bf16[8,32,384]{2,1,0:T(8,128)(2,1)S(1)} %slice_bitcast_fusion.query_ref, bf16[2,8192,384]{2,1,0:T(8,128)(2,1)} %bitcast.18), custom_call_target="tpu_custom_call" | custom-call | flops 3221225472 | bytes 6291456 | tf_op jit(solution)/shard_map/stale_attention/pallas_call | solution.py:107
  41.3 3.5 %collective-permute-done.rest_1_ = bf16[8,2,32,384]{3,2,1,0:T(8,128)(2,1)S(1)} collective-permute-done((bf16[8,2,32,384]{3,2,1,0:T(8,128)(2,1)S(1)}, bf16[8,2,32,384]{3,2,1,0:T(8,128)(2,1)S(1)}, u32[]{:S(2)}, u32[]{:S(2)}) %collective-permute-start) | collective-permute-done | bytes 393248 | tf_op jit(solution)/shard_map/ppermute | solution.py:177
  44.7 5.5 %collective-permute-done.1.rest_2_ = bf16[8,2,32,384]{3,2,1,0:T(8,128)(2,1)S(1)} collective-permute-done((bf16[8,2,32,384]{3,2,1,0:T(8,128)(2,1)S(1)}, bf16[8,2,32,384]{3,2,1,0:T(8,128)(2,1)S(1)}, u32[]{:S(2)}, u32[]{:S(2)}) %collective-permute-start.1) | collective-permute-done | bytes 393248 | tf_op jit(solution)/shard_map/ppermute | solution.py:177
  50.3 0.0 collective-permute-start.4
  50.3 0.5 collective-permute-start.5
  50.8 6.1 %stale_attention.3 = (f32[3,256,128]{2,1,0:T(8,128)S(1)}, f32[3,256,128]{2,1,0:T(8,128)S(1)}, f32[3,256,128]{2,1,0:T(8,128)S(1)}) custom-call(s32[1]{0:T(128)} %bitcast.me_ref, s32[32]{0:T(128)S(1)} %copy-done, s32[1,6]{1,0:T(1,128)S(1)} %copy-done.1, bf16[8,32,384]{2,1,0:T(8,128)(2,1)S(1)} %slice_bitcast_fusion.query_ref, bf16[2,8192,384]{2,1,0:T(8,128)(2,1)} %bitcast.19, ...), custom_call_target="tpu_custom_call" | custom-call | flops 3019898880 | bytes 5898240 | tf_op jit(solution)/shard_map/stale_attention/pallas_call | solution.py:107
  56.9 0.0 collective-permute-done.2.rest_3_
  56.9 0.0 collective-permute-done.3.rest_4_
  56.9 0.0 collective-permute-done.4.rest_5_
  57.0 0.0 collective-permute-done.5.rest_6_
  57.0 3.1 %fresh_attention.1 = bf16[8,32,384]{2,1,0:T(8,128)(2,1)S(1)} custom-call(s32[1]{0:T(128)} %bitcast.me_ref, s32[32]{0:T(128)S(1)} %copy-done, s32[1,6]{1,0:T(1,128)S(1)} %copy-done.1, bf16[8,32,384]{2,1,0:T(8,128)(2,1)S(1)} %slice_bitcast_fusion.query_ref, f32[3,256,128]{2,1,0:T(8,128)S(1)} %get-tuple-element.26.top_in, ...), custom_call_target="tpu_custom_call" | custom-call | tf_op jit(solution)/shard_map/fresh_attention/pallas_call | solution.py:164
  60.0 14.3 %all_to_all.10 = bf16[8,32,384]{2,1,0:T(8,128)(2,1)S(1)} all-to-all(bf16[8,32,384]{2,1,0:T(8,128)(2,1)S(1)} %fresh_attention.1), channel_id=1, replica_groups=mesh['pipe'=32,'uly'=8] {'uly'}, dimensions={0} | all-to-all | bytes 393216 | tf_op jit(solution)/shard_map/all_to_all | solution.py:181
  74.3 0.7 copy.10
  (2 shorter events, 0.1 us)
Async XLA Ops:
  2.0 27.4 %all-to-all-start = ((bf16[8,3,32,384]{3,2,1,0:T(8,128)(2,1)}), bf16[8,3,32,384]{3,2,1,0:T(8,128)(2,1)S(1)}, u32[]{:S(2)}, u32[]{:S(2)}) async-start(bf16[8,3,32,384]{3,2,1,0:T(8,128)(2,1)} %bitcast.17), calls=%async_computation | async-start | bytes 1179648 | tf_op jit(solution)/shard_map/all_to_all | solution.py:181
  10.4 23.4 %copy-start = (s32[32]{0:T(128)S(1)}, s32[32]{0:T(128)}, u32[]{:S(2)}) copy-start(s32[32]{0:T(128)} %plan_ref.5) | copy-start | bytes 388
  10.4 23.4 %copy-start.1 = (s32[1,6]{1,0:T(1,128)S(1)}, s32[1,6]{1,0:T(1,128)}, u32[]{:S(2)}) copy-start(s32[1,6]{1,0:T(1,128)} %refresh_ref.5) | copy-start | bytes 76
  29.4 15.3 %collective-permute-start = (bf16[8,2,32,384]{3,2,1,0:T(8,128)(2,1)S(1)}, bf16[8,2,32,384]{3,2,1,0:T(8,128)(2,1)S(1)}, u32[]{:S(2)}, u32[]{:S(2)}) collective-permute-start(bf16[8,2,32,384]{3,2,1,0:T(8,128)(2,1)S(1)} %slice.7.rest_0_), channel_id=1, source_target_pairs={{0,16},{8,24},{16,32},{24,40},{32,48},{40,56},{48,64},{56,72},{64,... | collective-permute-start | bytes 1179656 | tf_op jit(solution)/shard_map/ppermute | solution.py:177
  30.6 19.6 %collective-permute-start.1 = (bf16[8,2,32,384]{3,2,1,0:T(8,128)(2,1)S(1)}, bf16[8,2,32,384]{3,2,1,0:T(8,128)(2,1)S(1)}, u32[]{:S(2)}, u32[]{:S(2)}) collective-permute-start(bf16[8,2,32,384]{3,2,1,0:T(8,128)(2,1)S(1)} %slice.7.rest_0_), channel_id=1, source_target_pairs={{0,240},{8,248},{16,0},{24,8},{32,16},{40,24},{48,32},{56,40},{64,... | collective-permute-start | bytes 1179656 | tf_op jit(solution)/shard_map/ppermute | solution.py:177
  31.5 25.4 %collective-permute-start.2 = (bf16[8,2,32,384]{3,2,1,0:T(8,128)(2,1)S(1)}, bf16[8,2,32,384]{3,2,1,0:T(8,128)(2,1)S(1)}, u32[]{:S(2)}, u32[]{:S(2)}) collective-permute-start(bf16[8,2,32,384]{3,2,1,0:T(8,128)(2,1)S(1)} %slice.7.rest_0_), channel_id=1, source_target_pairs={{0,232},{8,32},{16,248},{24,48},{32,8},{40,64},{48,24},{56,80},{64... | collective-permute-start | bytes 1179656 | tf_op jit(solution)/shard_map/ppermute | solution.py:177
  31.9 25.0 %collective-permute-start.3 = (bf16[8,2,32,384]{3,2,1,0:T(8,128)(2,1)S(1)}, bf16[8,2,32,384]{3,2,1,0:T(8,128)(2,1)S(1)}, u32[]{:S(2)}, u32[]{:S(2)}) collective-permute-start(bf16[8,2,32,384]{3,2,1,0:T(8,128)(2,1)S(1)} %slice.7.rest_0_), channel_id=1, source_target_pairs={{0,8},{8,0},{16,24},{24,16},{32,40},{40,32},{48,56},{56,48},{64,72... | collective-permute-start | bytes 1179656 | tf_op jit(solution)/shard_map/ppermute | solution.py:177
  50.3 6.7 %collective-permute-start.4 = (bf16[8,2,32,384]{3,2,1,0:T(8,128)(2,1)S(1)}, bf16[8,2,32,384]{3,2,1,0:T(8,128)(2,1)S(1)}, u32[]{:S(2)}, u32[]{:S(2)}) collective-permute-start(bf16[8,2,32,384]{3,2,1,0:T(8,128)(2,1)S(1)} %collective-permute-done.rest_1_), channel_id=1, source_target_pairs={{0,8},{8,0},{16,24},{24,16},{32,40},{40,32},{48,56},{56,48},{64,72... | collective-permute-start | bytes 1179656 | tf_op jit(solution)/shard_map/ppermute | solution.py:177
  50.3 6.7 %collective-permute-start.5 = (bf16[8,2,32,384]{3,2,1,0:T(8,128)(2,1)S(1)}, bf16[8,2,32,384]{3,2,1,0:T(8,128)(2,1)S(1)}, u32[]{:S(2)}, u32[]{:S(2)}) collective-permute-start(bf16[8,2,32,384]{3,2,1,0:T(8,128)(2,1)S(1)} %collective-permute-done.1.rest_2_), channel_id=1, source_target_pairs={{0,8},{8,0},{16,24},{24,16},{32,40},{40,32},{48,56},{56,48},{64,72... | collective-permute-start | bytes 1179656 | tf_op jit(solution)/shard_map/ppermute | solution.py:177

commit v2 on v0

v2 whole, which is shorter than its diff:
```python
import math

import jax
import jax.numpy as jnp
from jax import lax
from jax.experimental import pallas as pl
from jax.experimental.pallas import tpu as pltpu
from jax.sharding import PartitionSpec as P

HD = 128
PT = 256
LOCAL = 3
WIDE = LOCAL * HD
PATCHES = 32
SLOTS = 6
SCALE = math.log2(math.e) / math.sqrt(HD)
GROUP = 6
FIRST = 24
VMEM_BYTES = 50 * 1024 * 1024


def columns(head):
    return slice(head * HD, (head + 1) * HD)


def absorb(head, scores, values, biases, top_ref, sum_ref, acc_ref):
    before = top_ref[head]
    top = before
    for score, bias in zip(scores, biases):
        widest = score[:, :HD]
        for start in range(HD, PT, HD):
            widest = jnp.maximum(widest, score[:, start:start + HD])
        widest = widest * SCALE
        top = jnp.maximum(top, widest if bias is None else widest + bias)
    top = jnp.broadcast_to(jnp.max(top, axis=1, keepdims=True), top.shape)
    fade = jnp.exp2(before - top)
    total = sum_ref[head] * fade
    mixed = acc_ref[head] * fade
    for score, value, bias in zip(scores, values, biases):
        level = top if bias is None else top - bias
        parts = []
        for start in range(0, PT, HD):
            probs = jnp.exp2(score[:, start:start + HD] * SCALE - level)
            total = total + probs
            parts.append(probs.astype(jnp.bfloat16))
        weights = jnp.concatenate(parts, axis=1)
        mixed = mixed + jnp.dot(weights, value, preferred_element_type=jnp.float32)
    acc_ref[head] = mixed
    sum_ref[head] = total
    top_ref[head] = top


def attend(query_ref, readers, biases, state):
    scores = []
    for head in range(LOCAL):
        query = query_ref[:, :, columns(head)].reshape(PT, HD)
        scores.append([
            lax.dot_general(query, read(0, head), (((1,), (1,)), ((), ())), preferred_element_type=jnp.float32)
            for read in readers
        ])
    for head in range(LOCAL):
        absorb(head, scores[head], [read(1, head) for read in readers], biases, *state)


def cached(held, place):
    return lambda part, head: held[part, place, :, columns(head)]


def moved(block_ref):
    return lambda part, head: block_ref[:, part, :, columns(head)].reshape(PT, HD)


def listing(patch, refresh_ref):
    found = refresh_ref[0, 0] == patch
    for slot in range(1, SLOTS):
        found = jnp.logical_or(found, refresh_ref[0, slot] == patch)
    return found


def bias_of(section, plan_ref, refresh_ref):
    patch = plan_ref[(section + PATCHES) % PATCHES]
    return jnp.where(listing(patch, refresh_ref), 0.0, -jnp.inf).astype(jnp.float32)


def fetch_stale(least, most, me_ref, plan_ref, refresh_ref, cache_ref, held, arrived):
    own = plan_ref[me_ref[0]]
    count = jnp.int32(0)
    for patch in range(PATCHES):
        stale = jnp.logical_not(jnp.logical_or(own == patch, listing(patch, refresh_ref)))

        @pl.when(stale & (count >= least) & (count < most))
        def _(patch=patch, place=count - least):
            pltpu.make_async_copy(
                cache_ref.at[:, pl.ds(patch * PT, PT), :], held.at[:, place], arrived.at[place]
            ).start()

        count = count + jnp.where(stale, 1, 0)
    return count


def attend_stale(first, width, query_ref, cache_ref, held, arrived, state):
    for place in range(width):
        pltpu.make_async_copy(
            cache_ref.at[:, pl.ds(0, PT), :], held.at[:, first + place], arrived.at[first + place]
        ).wait()
    attend(query_ref, [cached(held, first + place) for place in range(width)], [None] * width, state)


def sign_of(me):
    return jnp.where(me % 2 == 0, 1, -1)


def first_kernel(me_ref, plan_ref, refresh_ref, cache_ref, query_ref, top_ref, sum_ref, acc_ref, held, arrived):
    fetch_stale(0, FIRST, me_ref, plan_ref, refresh_ref, cache_ref, held, arrived)
    state = (top_ref, sum_ref, acc_ref)
    for target, value in zip(state, (-jnp.inf, 0.0, 0.0)):
        target[...] = jnp.full(target.shape, value, jnp.float32)

    @pl.loop(0, FIRST // GROUP)
    def _(group):
        attend_stale(group * GROUP, GROUP, query_ref, cache_ref, held, arrived, state)


def second_kernel(me_ref, plan_ref, refresh_ref, cache_ref, query_ref, top_in, sum_in, acc_in, own_ref, beside_ref,
                  behind_ref, ahead_ref, top_ref, sum_ref, acc_ref, held, arrived):
    left = fetch_stale(FIRST, PATCHES - 1, me_ref, plan_ref, refresh_ref, cache_ref, held, arrived) - FIRST
    state = (top_ref, sum_ref, acc_ref)
    for source, target in zip((top_in, sum_in, acc_in), state):
        target[...] = source[...]
    me = me_ref[0]
    biases = [None] + [
        bias_of(section, plan_ref, refresh_ref) for section in (me + sign_of(me), me - 2, me + 2)
    ]
    readers = [moved(block) for block in (own_ref, beside_ref, behind_ref, ahead_ref)]
    attend(query_ref, readers, biases, state)

    @pl.when(left >= 4)
    def _():
        attend_stale(0, 4, query_ref, cache_ref, held, arrived, state)

    done = jnp.where(left >= 4, 4, 0)
    for width in range(1, 4):

        @pl.when(left - done == width)
        def _(width=width):
            attend_stale(done, width, query_ref, cache_ref, held, arrived, state)


def last_kernel(me_ref, plan_ref, refresh_ref, query_ref, top_in, sum_in, acc_in, far_ref, beside_behind_ref,
                beside_ahead_ref, out_ref, top_ref, sum_ref, acc_ref):
    state = (top_ref, sum_ref, acc_ref)
    for source, target in zip((top_in, sum_in, acc_in), state):
        target[...] = source[...]
    me = me_ref[0]
    sign = sign_of(me)
    biases = [
        bias_of(section, plan_ref, refresh_ref) for section in (me - 3 * sign, me + sign - 2, me + sign + 2)
    ]
    readers = [moved(block) for block in (far_ref, beside_behind_ref, beside_ahead_ref)]
    attend(query_ref, readers, biases, state)
    for head in range(LOCAL):
        total = jnp.sum(sum_ref[head], axis=1, keepdims=True)
        done = (acc_ref[head] / total).astype(jnp.bfloat16)
        out_ref[:, :, columns(head)] = done.reshape(out_ref.shape[0], out_ref.shape[1], HD)


SMEM_SPEC = pl.BlockSpec(memory_space=pltpu.SMEM)
VMEM_SPEC = pl.BlockSpec(memory_space=pltpu.VMEM)
STATE = (jax.ShapeDtypeStruct((LOCAL, PT, HD), jnp.float32),) * 3


def patches(count):
    return [pltpu.VMEM((2, count, PT, WIDE), jnp.bfloat16), pltpu.SemaphoreType.DMA((count,))]


def run(kernel, blocks, scalars, arrays, out_shape, scratch, cache=()):
    keys = blocks * PT
    return pl.pallas_call(
        kernel,
        out_shape=out_shape,
        in_specs=[SMEM_SPEC] * len(scalars) + [pl.BlockSpec(memory_space=pl.ANY)] * len(cache) + [VMEM_SPEC] * len(arrays),
        out_specs=jax.tree.map(lambda _: VMEM_SPEC, out_shape),
        scratch_shapes=scratch,
        compiler_params=pltpu.CompilerParams(vmem_limit_bytes=VMEM_BYTES),
        cost_estimate=pl.CostEstimate(
            flops=8 * LOCAL * PT * keys * HD, bytes_accessed=2 * keys * WIDE * 2, transcendentals=LOCAL * PT * keys
        ),
    )(*scalars, *cache, *arrays)


def move(value, target):
    count = lax.axis_size("pipe")
    return lax.ppermute(value, "pipe", [(source, target(source) % count) for source in range(count)])


def exchange(value):
    return lax.all_to_all(value, "uly", split_axis=0, concat_axis=0, tiled=True)


def shards(fresh_qkv, stale_cache, plan, refresh):
    rows = fresh_qkv.shape[0]
    devices = lax.axis_size("uly")
    me = lax.axis_index("pipe").astype(jnp.int32)
    scalars = (me.reshape(1), plan, refresh)
    outgoing = fresh_qkv.reshape(rows, 3, devices, WIDE).transpose(2, 1, 0, 3)
    heads = exchange(outgoing)
    cache = stale_cache[0].transpose(1, 0, 2)
    heads, cache = lax.optimization_barrier((heads, cache))
    own, query = heads[:, 1:3], heads[:, 0]
    twin = lambda s: s ^ 1
    behind = move(own, lambda s: s + 2)
    ahead = move(own, lambda s: s - 2)
    beside = move(own, twin)
    state = run(first_kernel, FIRST, scalars, (query,), STATE, patches(FIRST), (cache,))
    state, behind, ahead = lax.optimization_barrier((state, behind, ahead))
    beside_behind = move(behind, twin)
    beside_ahead = move(ahead, twin)
    far = move(jnp.where(me % 2 == 1, behind, ahead), lambda s: s + 1 if s % 2 else s - 1)
    state = run(
        second_kernel, 8, scalars, (query, *state, own, beside, behind, ahead), STATE,
        patches(PATCHES - 1 - FIRST), (cache,),
    )
    held = pltpu.VMEM((LOCAL, PT, HD), jnp.float32)
    mixed = run(
        last_kernel, 3, scalars, (query, *state, far, beside_behind, beside_ahead),
        jax.ShapeDtypeStruct(query.shape, jnp.bfloat16), [held] * 3,
    )
    back = exchange(mixed)
    return back.transpose(1, 0, 2).reshape(rows, devices * WIDE)


def solution(mesh):
    placed = (P(("pipe", "uly"), None, None), P("pipe", None, None, "uly"), P(), P("pipe", None))
    return jax.shard_map(
        shards, mesh=mesh, in_specs=placed, out_specs=P(("pipe", "uly"), None), check_vma=False
    )
```

time: 180 us -> 69.5 us (0.39)
  the two profiles are of different devices: /device:TPU:30 before, /device:TPU:32 now
where the time goes in v2:
time: 69.5 us; the launch traced here: 69.1 us
  Pallas kernels  17.4 us (25%)
  starting transfers between devices  16.6 us (24%)
  local copies, waits for them, and re-layouts  14.4 us (21%)
  blocking collectives  12.2 us (18%)
  waiting for transfers between devices  8.38 us (12%)
    pallas_call x3, Pallas kernels, run(): pl.pallas_call(kernel, out_shape=out_shape, in_specs=[SMEM_SPEC] * len(sc...  17.4 us
    all_to_all x1, blocking collectives, exchange(): return lax.all_to_all(value, 'uly', split_axis=0, concat_axis=0, tiled=True)  12.2 us
    unnamed x7, local copies, waits for them, and re-layouts  11.7 us
    all_to_all x1, starting transfers between devices, exchange(): return lax.all_to_all(value, 'uly', split_axis=0, concat_axis=0, tiled=True)  8.57 us
    ppermute x6, starting transfers between devices, move(): lax.ppermute(value, 'pipe', [(source, target(source) % count) for source...  8.02 us
    all_to_all x1, waiting for transfers between devices, exchange(): return lax.all_to_all(value, 'uly', split_axis=0, concat_axis=0, tiled=True)  5.79 us
    ppermute x6, waiting for transfers between devices, move(): lax.ppermute(value, 'pipe', [(source, target(source) % count) for source...  2.59 us
    reshape x1, local copies, waits for them, and re-layouts, shards(): outgoing = fresh_qkv.reshape(rows, 3, devices, WIDE).transpose(2, 1, 0, 3)  1.98 us
  transfers between devices with their start and end apart: 7, of which 2 were waited for; matrix products, arithmetic and copies ran while one was open for 17% of the time, Pallas kernels for 23%

profile of v2, /device:TPU:32, one launch (start us, length us, event | category | flops | bytes accessed | tf_op | source)
XLA Modules:
  0.0 69.1 jit_solution(5014465926940990659)
XLA Ops:
  0.0 2.0 %copy.14 = bf16[3,4,8,8,384]{4,3,1,0,2:T(8,128)(2,1)} copy(bf16[3,4,8,8,384]{4,3,2,1,0:T(8,128)(2,1)} %bitcast.21) | data formatting | bytes 1179648 | tf_op jit(solution)/shard_map/reshape | solution.py:205
  2.0 8.6 %all-to-all-start = ((bf16[8,3,32,384]{3,2,1,0:T(8,128)(2,1)}), bf16[8,3,32,384]{3,2,1,0:T(8,128)(2,1)S(1)}, u32[]{:S(2)}, u32[]{:S(2)}) async-start(bf16[8,3,32,384]{3,2,1,0:T(8,128)(2,1)} %bitcast.17), calls=%async_computation | async-start | bytes 1179648 | tf_op jit(solution)/shard_map/all_to_all | solution.py:197
  10.6 0.0 copy-start
  10.6 0.0 copy-start.1
  10.6 11.6 %copy.13 = bf16[1,8192,2,384]{3,1,2,0:T(8,128)(2,1)} copy(bf16[1,8192,2,384]{3,2,1,0:T(2,128)(2,1)} %param.5) | data formatting | bytes 25165824 | tf_op args[1]
  22.2 5.8 %all-to-all-done = bf16[8,3,32,384]{3,2,1,0:T(8,128)(2,1)S(1)} async-done(((bf16[8,3,32,384]{3,2,1,0:T(8,128)(2,1)}), bf16[8,3,32,384]{3,2,1,0:T(8,128)(2,1)S(1)}, u32[]{:S(2)}, u32[]{:S(2)}) %all-to-all-start) | async-done | bytes 589856 | tf_op jit(solution)/shard_map/all_to_all | solution.py:197
  28.1 1.7 %collective-permute-start = (bf16[8,2,32,384]{3,2,1,0:T(8,128)(2,1)S(1)}, bf16[8,2,32,384]{3,2,1,0:T(8,128)(2,1)S(1)}, u32[]{:S(2)}, u32[]{:S(2)}) collective-permute-start(bf16[8,2,32,384]{3,2,1,0:T(8,128)(2,1)S(1)} %slice.7.own_ref), channel_id=1, source_target_pairs={{0,16},{8,24},{16,32},{24,40},{32,48},{40,56},{48,64},{56,72},{64,... | collective-permute-start | bytes 1179656 | tf_op jit(solution)/shard_map/ppermute | solution.py:193
  29.7 3.8 %collective-permute-start.1 = (bf16[8,2,32,384]{3,2,1,0:T(8,128)(2,1)S(1)}, bf16[8,2,32,384]{3,2,1,0:T(8,128)(2,1)S(1)}, u32[]{:S(2)}, u32[]{:S(2)}) collective-permute-start(bf16[8,2,32,384]{3,2,1,0:T(8,128)(2,1)S(1)} %slice.7.own_ref), channel_id=1, source_target_pairs={{0,240},{8,248},{16,0},{24,8},{32,16},{40,24},{48,32},{56,40},{64,... | collective-permute-start | bytes 1179656 | tf_op jit(solution)/shard_map/ppermute | solution.py:193
  33.5 0.0 collective-permute-start.2
  33.5 0.0 copy-done
  33.5 0.0 copy-done.1
  33.5 10.1 %shard_map.46 = (f32[3,256,128]{2,1,0:T(8,128)S(1)}, f32[3,256,128]{2,1,0:T(8,128)S(1)}, f32[3,256,128]{2,1,0:T(8,128)S(1)}) custom-call(s32[1]{0:T(128)} %bitcast.me_ref, s32[32]{0:T(128)S(1)} %copy-done, s32[1,6]{1,0:T(1,128)S(1)} %copy-done.1, bf16[2,8192,384]{2,1,0:T(8,128)(2,1)} %bitcast.18, bf16[8,32,384]{2,1,0:T(8,128)(2,1)S(1)} %slice_bitcast_fusion.query_ref), custom_call_target="tpu_custom_call" | custom-call | flops 4831838208 | bytes 9437184 | tf_op jit(solution)/shard_map/pallas_call | solution.py:178
  43.7 0.0 collective-permute-done.behind_ref
  43.7 0.0 collective-permute-done.1.ahead_ref
  43.7 0.0 copy-start.2
  43.7 0.1 broadcast_select_fusion
  43.8 2.1 %collective-permute-start.3 = (bf16[8,2,32,384]{3,2,1,0:T(8,128)(2,1)S(1)}, bf16[8,2,32,384]{3,2,1,0:T(8,128)(2,1)S(1)}, u32[]{:S(2)}, u32[]{:S(2)}) collective-permute-start(bf16[8,2,32,384]{3,2,1,0:T(8,128)(2,1)S(1)} %broadcast_select_fusion), channel_id=1, source_target_pairs={{0,248},{8,16},{16,8},{24,32},{32,24},{40,48},{48,40},{56,64},{64,... | collective-permute-start | bytes 1179656 | tf_op jit(solution)/shard_map/ppermute | solution.py:193
  45.9 0.0 collective-permute-start.4
  45.9 0.5 collective-permute-start.5
  46.4 0.0 collective-permute-done.2.beside_ref
  46.4 0.0 copy-done.2
  46.4 5.4 %shard_map.47 = (f32[3,256,128]{2,1,0:T(8,128)S(1)}, f32[3,256,128]{2,1,0:T(8,128)S(1)}, f32[3,256,128]{2,1,0:T(8,128)S(1)}) custom-call(s32[1]{0:T(128)} %bitcast.me_ref, s32[32]{0:T(128)S(1)} %copy-done, s32[1,6]{1,0:T(1,128)S(1)} %copy-done.1, bf16[2,8192,384]{2,1,0:T(8,128)(2,1)} %bitcast.19, bf16[8,32,384]{2,1,0:T(8,128)(2,1)S(1)} %slice_bitcast_fusion.query_ref, ...), custom_call_target="tpu_custom_call" | custom-call | flops 1610612736 | bytes 3145728 | tf_op jit(solution)/shard_map/pallas_call | solution.py:178
  51.8 2.6 %collective-permute-done.3.far_ref = bf16[8,2,32,384]{3,2,1,0:T(8,128)(2,1)S(1)} collective-permute-done((bf16[8,2,32,384]{3,2,1,0:T(8,128)(2,1)S(1)}, bf16[8,2,32,384]{3,2,1,0:T(8,128)(2,1)S(1)}, u32[]{:S(2)}, u32[]{:S(2)}) %collective-permute-start.3) | collective-permute-done | bytes 393248 | tf_op jit(solution)/shard_map/ppermute | solution.py:193
  54.4 0.0 collective-permute-done.4.beside_behind_ref
  54.4 0.0 collective-permute-done.5.beside_ahead_ref
  54.4 1.8 %shard_map.48 = bf16[8,32,384]{2,1,0:T(8,128)(2,1)S(1)} custom-call(s32[1]{0:T(128)} %bitcast.me_ref, s32[32]{0:T(128)S(1)} %copy-done, s32[1,6]{1,0:T(1,128)S(1)} %copy-done.1, bf16[8,32,384]{2,1,0:T(8,128)(2,1)S(1)} %slice_bitcast_fusion.query_ref, f32[3,256,128]{2,1,0:T(8,128)S(1)} %get-tuple-element.28.top_in, ...), custom_call_target="tpu_custom_call" | custom-call | flops 603979776 | bytes 1179648 | tf_op jit(solution)/shard_map/pallas_call | solution.py:178
  56.2 12.2 %all_to_all.10 = bf16[8,32,384]{2,1,0:T(8,128)(2,1)S(1)} all-to-all(bf16[8,32,384]{2,1,0:T(8,128)(2,1)S(1)} %shard_map.48), channel_id=1, replica_groups=mesh['pipe'=32,'uly'=8] {'uly'}, dimensions={0} | all-to-all | bytes 393216 | tf_op jit(solution)/shard_map/all_to_all | solution.py:197
  68.4 0.7 %copy.10 = bf16[8,4,8,384]{3,2,0,1:T(8,128)(2,1)} copy(bf16[8,4,8,384]{3,2,1,0:T(8,128)(2,1)S(1)} %bitcast.20) | data formatting | bytes 393216 | tf_op jit(solution)/shard_map/reshape | solution.py:229
  (2 shorter events, 0.1 us)
Async XLA Ops:
  2.0 26.0 %all-to-all-start = ((bf16[8,3,32,384]{3,2,1,0:T(8,128)(2,1)}), bf16[8,3,32,384]{3,2,1,0:T(8,128)(2,1)S(1)}, u32[]{:S(2)}, u32[]{:S(2)}) async-start(bf16[8,3,32,384]{3,2,1,0:T(8,128)(2,1)} %bitcast.17), calls=%async_computation | async-start | bytes 1179648 | tf_op jit(solution)/shard_map/all_to_all | solution.py:197
  10.6 23.0 %copy-start = (s32[32]{0:T(128)S(1)}, s32[32]{0:T(128)}, u32[]{:S(2)}) copy-start(s32[32]{0:T(128)} %plan_ref.5) | copy-start | bytes 388
  10.6 23.0 %copy-start.1 = (s32[1,6]{1,0:T(1,128)S(1)}, s32[1,6]{1,0:T(1,128)}, u32[]{:S(2)}) copy-start(s32[1,6]{1,0:T(1,128)} %refresh_ref.5) | copy-start | bytes 76
  28.1 15.6 %collective-permute-start = (bf16[8,2,32,384]{3,2,1,0:T(8,128)(2,1)S(1)}, bf16[8,2,32,384]{3,2,1,0:T(8,128)(2,1)S(1)}, u32[]{:S(2)}, u32[]{:S(2)}) collective-permute-start(bf16[8,2,32,384]{3,2,1,0:T(8,128)(2,1)S(1)} %slice.7.own_ref), channel_id=1, source_target_pairs={{0,16},{8,24},{16,32},{24,40},{32,48},{40,56},{48,64},{56,72},{64,... | collective-permute-start | bytes 1179656 | tf_op jit(solution)/shard_map/ppermute | solution.py:193
  29.7 13.9 %collective-permute-start.1 = (bf16[8,2,32,384]{3,2,1,0:T(8,128)(2,1)S(1)}, bf16[8,2,32,384]{3,2,1,0:T(8,128)(2,1)S(1)}, u32[]{:S(2)}, u32[]{:S(2)}) collective-permute-start(bf16[8,2,32,384]{3,2,1,0:T(8,128)(2,1)S(1)} %slice.7.own_ref), channel_id=1, source_target_pairs={{0,240},{8,248},{16,0},{24,8},{32,16},{40,24},{48,32},{56,40},{64,... | collective-permute-start | bytes 1179656 | tf_op jit(solution)/shard_map/ppermute | solution.py:193
  33.5 12.9 %collective-permute-start.2 = (bf16[8,2,32,384]{3,2,1,0:T(8,128)(2,1)S(1)}, bf16[8,2,32,384]{3,2,1,0:T(8,128)(2,1)S(1)}, u32[]{:S(2)}, u32[]{:S(2)}) collective-permute-start(bf16[8,2,32,384]{3,2,1,0:T(8,128)(2,1)S(1)} %slice.7.own_ref), channel_id=1, source_target_pairs={{0,8},{8,0},{16,24},{24,16},{32,40},{40,32},{48,56},{56,48},{64,72... | collective-permute-start | bytes 1179656 | tf_op jit(solution)/shard_map/ppermute | solution.py:193
  43.7 2.7 %copy-start.2 = (bf16[8,2,32,384]{3,2,1,0:T(8,128)(2,1)}, bf16[8,2,32,384]{3,2,1,0:T(8,128)(2,1)S(1)}, u32[]{:S(2)}) copy-start(bf16[8,2,32,384]{3,2,1,0:T(8,128)(2,1)S(1)} %collective-permute-done.1.ahead_ref) | copy-start | bytes 1179652
  43.8 10.6 %collective-permute-start.3 = (bf16[8,2,32,384]{3,2,1,0:T(8,128)(2,1)S(1)}, bf16[8,2,32,384]{3,2,1,0:T(8,128)(2,1)S(1)}, u32[]{:S(2)}, u32[]{:S(2)}) collective-permute-start(bf16[8,2,32,384]{3,2,1,0:T(8,128)(2,1)S(1)} %broadcast_select_fusion), channel_id=1, source_target_pairs={{0,248},{8,16},{16,8},{24,32},{32,24},{40,48},{48,40},{56,64},{64,... | collective-permute-start | bytes 1179656 | tf_op jit(solution)/shard_map/ppermute | solution.py:193
  45.9 8.5 %collective-permute-start.4 = (bf16[8,2,32,384]{3,2,1,0:T(8,128)(2,1)S(1)}, bf16[8,2,32,384]{3,2,1,0:T(8,128)(2,1)S(1)}, u32[]{:S(2)}, u32[]{:S(2)}) collective-permute-start(bf16[8,2,32,384]{3,2,1,0:T(8,128)(2,1)S(1)} %collective-permute-done.behind_ref), channel_id=1, source_target_pairs={{0,8},{8,0},{16,24},{24,16},{32,40},{40,32},{48,56},{56,48},{64,72... | collective-permute-start | bytes 1179656 | tf_op jit(solution)/shard_map/ppermute | solution.py:193
  45.9 8.5 %collective-permute-start.5 = (bf16[8,2,32,384]{3,2,1,0:T(8,128)(2,1)S(1)}, bf16[8,2,32,384]{3,2,1,0:T(8,128)(2,1)S(1)}, u32[]{:S(2)}, u32[]{:S(2)}) collective-permute-start(bf16[8,2,32,384]{3,2,1,0:T(8,128)(2,1)S(1)} %collective-permute-done.1.ahead_ref), channel_id=1, source_target_pairs={{0,8},{8,0},{16,24},{24,16},{32,40},{40,32},{48,56},{56,48},{64,72... | collective-permute-start | bytes 1179656 | tf_op jit(solution)/shard_map/ppermute | solution.py:193

commit v3 on v2

--- a/solution.py
+++ b/solution.py
@@ -82,48 +82,61 @@
     return jnp.where(listing(patch, refresh_ref), 0.0, -jnp.inf).astype(jnp.float32)
 
 
-def fetch_stale(least, most, me_ref, plan_ref, refresh_ref, cache_ref, held, arrived):
+def fetch(patch, place, cache_ref, held, arrived):
+    return pltpu.make_async_copy(
+        cache_ref.at[:, pl.ds(pl.multiple_of(patch * PT, PT), PT), :], held.at[:, place], arrived.at[place]
+    )
+
+
+def attend_stale(first, width, query_ref, cache_ref, held, arrived, state):
+    for place in range(width):
+        fetch(0, first + place, cache_ref, held, arrived).wait()
+    attend(query_ref, [cached(held, first + place) for place in range(width)], [None] * width, state)
+
+
+def sign_of(me):
+    return jnp.where(me % 2 == 0, 1, -1)
+
+
+def order_kernel(me_ref, plan_ref, refresh_ref, order_ref):
     own = plan_ref[me_ref[0]]
     count = jnp.int32(0)
     for patch in range(PATCHES):
-        stale = jnp.logical_not(jnp.logical_or(own == patch, listing(patch, refresh_ref)))
-
-        @pl.when(stale & (count >= least) & (count < most))
-        def _(patch=patch, place=count - least):
-            pltpu.make_async_copy(
-                cache_ref.at[:, pl.ds(patch * PT, PT), :], held.at[:, place], arrived.at[place]
-            ).start()
-
-        count = count + jnp.where(stale, 1, 0)
-    return count
-
-
-def attend_stale(first, width, query_ref, cache_ref, held, arrived, state):
-    for place in range(width):
-        pltpu.make_async_copy(
-            cache_ref.at[:, pl.ds(0, PT), :], held.at[:, first + place], arrived.at[first + place]
-        ).wait()
-    attend(query_ref, [cached(held, first + place) for place in range(width)], [None] * width, state)
-
-
-def sign_of(me):
-    return jnp.where(me % 2 == 0, 1, -1)
-
-
-def first_kernel(me_ref, plan_ref, refresh_ref, cache_ref, query_ref, top_ref, sum_ref, acc_ref, held, arrived):
-    fetch_stale(0, FIRST, me_ref, plan_ref, refresh_ref, cache_ref, held, arrived)
+        order_ref[count] = jnp.int32(patch)
+        fresh = jnp.logical_or(own == patch, listing(patch, refresh_ref))
+        count = count + jnp.where(fresh, 0, 1)
+    order_ref[PATCHES] = count
+
+
+def first_kernel(order_ref, cache_ref, query_ref, top_ref, sum_ref, acc_ref, held, arrived):
+    def begin(group):
+        for place in range(GROUP):
+            place = group * GROUP + place
+            fetch(order_ref[place], place, cache_ref, held, arrived).start()
+
+    begin(0)
+    begin(1)
     state = (top_ref, sum_ref, acc_ref)
     for target, value in zip(state, (-jnp.inf, 0.0, 0.0)):
         target[...] = jnp.full(target.shape, value, jnp.float32)
 
     @pl.loop(0, FIRST // GROUP)
     def _(group):
+        @pl.when(group + 2 < FIRST // GROUP)
+        def _():
+            begin(group + 2)
+
         attend_stale(group * GROUP, GROUP, query_ref, cache_ref, held, arrived, state)
 
 
-def second_kernel(me_ref, plan_ref, refresh_ref, cache_ref, query_ref, top_in, sum_in, acc_in, own_ref, beside_ref,
-                  behind_ref, ahead_ref, top_ref, sum_ref, acc_ref, held, arrived):
-    left = fetch_stale(FIRST, PATCHES - 1, me_ref, plan_ref, refresh_ref, cache_ref, held, arrived) - FIRST
+def second_kernel(me_ref, plan_ref, refresh_ref, order_ref, cache_ref, query_ref, top_in, sum_in, acc_in, own_ref,
+                  beside_ref, behind_ref, ahead_ref, top_ref, sum_ref, acc_ref, held, arrived):
+    left = order_ref[PATCHES] - FIRST
+
+    @pl.loop(0, left)
+    def _(place):
+        fetch(order_ref[FIRST + place], place, cache_ref, held, arrived).start()
+
     state = (top_ref, sum_ref, acc_ref)
     for source, target in zip((top_in, sum_in, acc_in), state):
         target[...] = source[...]
@@ -188,6 +201,15 @@
     )(*scalars, *cache, *arrays)
 
 
+def stale_order(scalars):
+    return pl.pallas_call(
+        order_kernel,
+        out_shape=jax.ShapeDtypeStruct((PATCHES + 1,), jnp.int32),
+        in_specs=[SMEM_SPEC] * 3,
+        out_specs=SMEM_SPEC,
+    )(*scalars)
+
+
 def move(value, target):
     count = lax.axis_size("pipe")
     return lax.ppermute(value, "pipe", [(source, target(source) % count) for source in range(count)])
@@ -205,19 +227,20 @@
     outgoing = fresh_qkv.reshape(rows, 3, devices, WIDE).transpose(2, 1, 0, 3)
     heads = exchange(outgoing)
     cache = stale_cache[0].transpose(1, 0, 2)
-    heads, cache = lax.optimization_barrier((heads, cache))
+    order = stale_order(scalars)
+    heads, cache, order = lax.optimization_barrier((heads, cache, order))
     own, query = heads[:, 1:3], heads[:, 0]
     twin = lambda s: s ^ 1
     behind = move(own, lambda s: s + 2)
     ahead = move(own, lambda s: s - 2)
     beside = move(own, twin)
-    state = run(first_kernel, FIRST, scalars, (query,), STATE, patches(FIRST), (cache,))
+    state = run(first_kernel, FIRST, (order,), (query,), STATE, patches(FIRST), (cache,))
     state, behind, ahead = lax.optimization_barrier((state, behind, ahead))
     beside_behind = move(behind, twin)
     beside_ahead = move(ahead, twin)
     far = move(jnp.where(me % 2 == 1, behind, ahead), lambda s: s + 1 if s % 2 else s - 1)
     state = run(
-        second_kernel, 8, scalars, (query, *state, own, beside, behind, ahead), STATE,
+        second_kernel, 8, (*scalars, order), (query, *state, own, beside, behind, ahead), STATE,
         patches(PATCHES - 1 - FIRST), (cache,),
     )
     held = pltpu.VMEM((LOCAL, PT, HD), jnp.float32)

time: 69.5 us -> 69.4 us (level)
  Pallas kernels: 17.4 us -> 16.3 us
    pallas_call x3, Pallas kernels: 17.4 us -> 14.8 us  [run(): pl.pallas_call(kernel, out_shape=out_shape, in_specs=[SMEM_SPEC] * len(sc...]
    ppermute x6, waiting for transfers between devices: 2.59 us -> 4.43 us  [move(): lax.ppermute(value, 'pipe', [(source, target(source) % count) for source...]
    pallas_call x0 -> x1, Pallas kernels: none -> 1.48 us  [stale_order(): pl.pallas_call(order_kernel, out_shape=jax.ShapeDtypeStruct((PATCHES + 1,...]
    all_to_all x1, waiting for transfers between devices: 5.79 us -> 4.41 us  [exchange(): return lax.all_to_all(value, 'uly', split_axis=0, concat_axis=0, tiled=True)]
    unnamed x7 -> x11, local copies, waits for them, and re-layouts: 11.7 us -> 12.2 us
  transfers between devices with their start and end apart: 7 -> 7, of which waited for: 2 -> 2; matrix products, arithmetic and copies ran while one was open for 17% -> 17% of each run, Pallas kernels for 23% -> 21%
where the time goes in v3:
time: 69.4 us; the launch traced here: 69 us
  starting transfers between devices  16.6 us (24%)
  Pallas kernels  16.3 us (23%)
  local copies, waits for them, and re-layouts  14.9 us (21%)
  blocking collectives  12.2 us (18%)
  waiting for transfers between devices  8.85 us (13%)
    pallas_call x3, Pallas kernels, run(): pl.pallas_call(kernel, out_shape=out_shape, in_specs=[SMEM_SPEC] * len(sc...  14.8 us
    unnamed x11, local copies, waits for them, and re-layouts  12.2 us
    all_to_all x1, blocking collectives, exchange(): return lax.all_to_all(value, 'uly', split_axis=0, concat_axis=0, tiled=True)  12.2 us
    all_to_all x1, starting transfers between devices, exchange(): return lax.all_to_all(value, 'uly', split_axis=0, concat_axis=0, tiled=True)  8.57 us
    ppermute x6, starting transfers between devices, move(): lax.ppermute(value, 'pipe', [(source, target(source) % count) for source...  8.02 us
    ppermute x6, waiting for transfers between devices, move(): lax.ppermute(value, 'pipe', [(source, target(source) % count) for source...  4.43 us
    all_to_all x1, waiting for transfers between devices, exchange(): return lax.all_to_all(value, 'uly', split_axis=0, concat_axis=0, tiled=True)  4.41 us
    reshape x1, local copies, waits for them, and re-layouts, shards(): outgoing = fresh_qkv.reshape(rows, 3, devices, WIDE).transpose(2, 1, 0, 3)  1.98 us
  transfers between devices with their start and end apart: 7, of which 2 were waited for; matrix products, arithmetic and copies ran while one was open for 17% of the time, Pallas kernels for 21%

profile of v3, /device:TPU:32, one launch (start us, length us, event | category | flops | bytes accessed | tf_op | source)
XLA Modules:
  0.0 69.0 jit_solution(18378356168611983088)
XLA Ops:
  0.0 2.0 %copy.14 = bf16[3,4,8,8,384]{4,3,1,0,2:T(8,128)(2,1)} copy(bf16[3,4,8,8,384]{4,3,2,1,0:T(8,128)(2,1)} %bitcast.21) | data formatting | bytes 1179648 | tf_op jit(solution)/shard_map/reshape | solution.py:227
  2.0 8.6 %all-to-all-start = ((bf16[8,3,32,384]{3,2,1,0:T(8,128)(2,1)}), bf16[8,3,32,384]{3,2,1,0:T(8,128)(2,1)S(1)}, u32[]{:S(2)}, u32[]{:S(2)}) async-start(bf16[8,3,32,384]{3,2,1,0:T(8,128)(2,1)} %bitcast.17), calls=%async_computation | async-start | bytes 1179648 | tf_op jit(solution)/shard_map/all_to_all | solution.py:219
  10.5 11.5 %copy.13 = bf16[1,8192,2,384]{3,1,2,0:T(8,128)(2,1)} copy(bf16[1,8192,2,384]{3,2,1,0:T(2,128)(2,1)} %param.5) | data formatting | bytes 25165824 | tf_op args[1]
  22.1 0.0 copy-start
  22.1 0.0 copy-start.1
  22.1 1.5 %shard_map.46.order_ref = s32[33]{0:T(128)} custom-call(s32[1]{0:T(128)} %bitcast.me_ref, s32[32]{0:T(128)} %plan_ref.5, s32[1,6]{1,0:T(1,128)} %refresh_ref.5), custom_call_target="tpu_custom_call" | custom-call | tf_op jit(solution)/shard_map/pallas_call | solution.py:205
  23.6 0.0 copy-start.3
  23.6 4.4 %all-to-all-done = bf16[8,3,32,384]{3,2,1,0:T(8,128)(2,1)S(1)} async-done(((bf16[8,3,32,384]{3,2,1,0:T(8,128)(2,1)}), bf16[8,3,32,384]{3,2,1,0:T(8,128)(2,1)S(1)}, u32[]{:S(2)}, u32[]{:S(2)}) %all-to-all-start) | async-done | bytes 589856 | tf_op jit(solution)/shard_map/all_to_all | solution.py:219
  28.1 1.7 %collective-permute-start = (bf16[8,2,32,384]{3,2,1,0:T(8,128)(2,1)S(1)}, bf16[8,2,32,384]{3,2,1,0:T(8,128)(2,1)S(1)}, u32[]{:S(2)}, u32[]{:S(2)}) collective-permute-start(bf16[8,2,32,384]{3,2,1,0:T(8,128)(2,1)S(1)} %slice.7.own_ref), channel_id=1, source_target_pairs={{0,16},{8,24},{16,32},{24,40},{32,48},{40,56},{48,64},{56,72},{64,... | collective-permute-start | bytes 1179656 | tf_op jit(solution)/shard_map/ppermute | solution.py:215
  29.7 3.8 %collective-permute-start.1 = (bf16[8,2,32,384]{3,2,1,0:T(8,128)(2,1)S(1)}, bf16[8,2,32,384]{3,2,1,0:T(8,128)(2,1)S(1)}, u32[]{:S(2)}, u32[]{:S(2)}) collective-permute-start(bf16[8,2,32,384]{3,2,1,0:T(8,128)(2,1)S(1)} %slice.7.own_ref), channel_id=1, source_target_pairs={{0,240},{8,248},{16,0},{24,8},{32,16},{40,24},{48,32},{56,40},{64,... | collective-permute-start | bytes 1179656 | tf_op jit(solution)/shard_map/ppermute | solution.py:215
  33.5 0.0 collective-permute-start.2
  33.5 0.7 copy-done.2
  34.2 9.6 %shard_map.47 = (f32[3,256,128]{2,1,0:T(8,128)S(1)}, f32[3,256,128]{2,1,0:T(8,128)S(1)}, f32[3,256,128]{2,1,0:T(8,128)S(1)}) custom-call(s32[33]{0:T(128)S(1)} %copy-done.2, bf16[2,8192,384]{2,1,0:T(8,128)(2,1)} %bitcast.18, bf16[8,32,384]{2,1,0:T(8,128)(2,1)S(1)} %slice_bitcast_fusion.query_ref), custom_call_target="tpu_custom_call" | custom-call | flops 4831838208 | bytes 9437184 | tf_op jit(solution)/shard_map/pallas_call | solution.py:191
  43.7 0.0 collective-permute-done.behind_ref
  43.7 0.0 collective-permute-done.1.ahead_ref
  43.7 0.0 copy-start.4
  43.7 0.1 broadcast_select_fusion
  43.8 2.1 %collective-permute-start.3 = (bf16[8,2,32,384]{3,2,1,0:T(8,128)(2,1)S(1)}, bf16[8,2,32,384]{3,2,1,0:T(8,128)(2,1)S(1)}, u32[]{:S(2)}, u32[]{:S(2)}) collective-permute-start(bf16[8,2,32,384]{3,2,1,0:T(8,128)(2,1)S(1)} %broadcast_select_fusion), channel_id=1, source_target_pairs={{0,248},{8,16},{16,8},{24,32},{32,24},{40,48},{48,40},{56,64},{64,... | collective-permute-start | bytes 1179656 | tf_op jit(solution)/shard_map/ppermute | solution.py:215
  45.9 0.0 collective-permute-start.4
  45.9 0.5 collective-permute-start.5
  46.4 0.0 collective-permute-done.2.beside_ref
  46.4 0.0 copy-done.4
  46.4 0.0 copy-done
  46.4 0.0 copy-done.1
  46.4 0.0 copy-done.3
  46.4 3.5 %shard_map.48 = (f32[3,256,128]{2,1,0:T(8,128)S(1)}, f32[3,256,128]{2,1,0:T(8,128)S(1)}, f32[3,256,128]{2,1,0:T(8,128)S(1)}) custom-call(s32[1]{0:T(128)} %bitcast.me_ref, s32[32]{0:T(128)S(1)} %copy-done, s32[1,6]{1,0:T(1,128)S(1)} %copy-done.1, s32[33]{0:T(128)S(1)} %copy-done.3, bf16[2,8192,384]{2,1,0:T(8,128)(2,1)} %bitcast.19, ...), custom_call_target="tpu_custom_call" | custom-call | flops 1610612736 | bytes 3145728 | tf_op jit(solution)/shard_map/pallas_call | solution.py:191
  50.0 4.4 %collective-permute-done.3.far_ref = bf16[8,2,32,384]{3,2,1,0:T(8,128)(2,1)S(1)} collective-permute-done((bf16[8,2,32,384]{3,2,1,0:T(8,128)(2,1)S(1)}, bf16[8,2,32,384]{3,2,1,0:T(8,128)(2,1)S(1)}, u32[]{:S(2)}, u32[]{:S(2)}) %collective-permute-start.3) | collective-permute-done | bytes 393248 | tf_op jit(solution)/shard_map/ppermute | solution.py:215
  54.4 0.0 collective-permute-done.4.beside_behind_ref
  54.4 0.0 collective-permute-done.5.beside_ahead_ref
  54.4 1.7 %shard_map.49 = bf16[8,32,384]{2,1,0:T(8,128)(2,1)S(1)} custom-call(s32[1]{0:T(128)} %bitcast.me_ref, s32[32]{0:T(128)S(1)} %copy-done, s32[1,6]{1,0:T(1,128)S(1)} %copy-done.1, bf16[8,32,384]{2,1,0:T(8,128)(2,1)S(1)} %slice_bitcast_fusion.query_ref, f32[3,256,128]{2,1,0:T(8,128)S(1)} %get-tuple-element.30.top_in, ...), custom_call_target="tpu_custom_call" | custom-call | flops 603979776 | bytes 1179648 | tf_op jit(solution)/shard_map/pallas_call | solution.py:191
  56.1 12.2 %all_to_all.10 = bf16[8,32,384]{2,1,0:T(8,128)(2,1)S(1)} all-to-all(bf16[8,32,384]{2,1,0:T(8,128)(2,1)S(1)} %shard_map.49), channel_id=1, replica_groups=mesh['pipe'=32,'uly'=8] {'uly'}, dimensions={0} | all-to-all | bytes 393216 | tf_op jit(solution)/shard_map/all_to_all | solution.py:219
  68.3 0.7 %copy.10 = bf16[8,4,8,384]{3,2,0,1:T(8,128)(2,1)} copy(bf16[8,4,8,384]{3,2,1,0:T(8,128)(2,1)S(1)} %bitcast.20) | data formatting | bytes 393216 | tf_op jit(solution)/shard_map/reshape | solution.py:252
  (3 shorter events, 0.1 us)
Async XLA Ops:
  2.0 26.0 %all-to-all-start = ((bf16[8,3,32,384]{3,2,1,0:T(8,128)(2,1)}), bf16[8,3,32,384]{3,2,1,0:T(8,128)(2,1)S(1)}, u32[]{:S(2)}, u32[]{:S(2)}) async-start(bf16[8,3,32,384]{3,2,1,0:T(8,128)(2,1)} %bitcast.17), calls=%async_computation | async-start | bytes 1179648 | tf_op jit(solution)/shard_map/all_to_all | solution.py:219
  22.1 24.4 %copy-start = (s32[32]{0:T(128)S(1)}, s32[32]{0:T(128)}, u32[]{:S(2)}) copy-start(s32[32]{0:T(128)} %plan_ref.5) | copy-start | bytes 388
  22.1 24.4 %copy-start.1 = (s32[1,6]{1,0:T(1,128)S(1)}, s32[1,6]{1,0:T(1,128)}, u32[]{:S(2)}) copy-start(s32[1,6]{1,0:T(1,128)} %refresh_ref.5) | copy-start | bytes 76
  23.6 22.9 %copy-start.3 = (s32[33]{0:T(128)S(1)}, s32[33]{0:T(128)}, u32[]{:S(2)}) copy-start(s32[33]{0:T(128)} %shard_map.46.order_ref) | copy-start | bytes 400
  28.1 15.7 %collective-permute-start = (bf16[8,2,32,384]{3,2,1,0:T(8,128)(2,1)S(1)}, bf16[8,2,32,384]{3,2,1,0:T(8,128)(2,1)S(1)}, u32[]{:S(2)}, u32[]{:S(2)}) collective-permute-start(bf16[8,2,32,384]{3,2,1,0:T(8,128)(2,1)S(1)} %slice.7.own_ref), channel_id=1, source_target_pairs={{0,16},{8,24},{16,32},{24,40},{32,48},{40,56},{48,64},{56,72},{64,... | collective-permute-start | bytes 1179656 | tf_op jit(solution)/shard_map/ppermute | solution.py:215
  29.7 14.0 %collective-permute-start.1 = (bf16[8,2,32,384]{3,2,1,0:T(8,128)(2,1)S(1)}, bf16[8,2,32,384]{3,2,1,0:T(8,128)(2,1)S(1)}, u32[]{:S(2)}, u32[]{:S(2)}) collective-permute-start(bf16[8,2,32,384]{3,2,1,0:T(8,128)(2,1)S(1)} %slice.7.own_ref), channel_id=1, source_target_pairs={{0,240},{8,248},{16,0},{24,8},{32,16},{40,24},{48,32},{56,40},{64,... | collective-permute-start | bytes 1179656 | tf_op jit(solution)/shard_map/ppermute | solution.py:215
  33.5 12.9 %collective-permute-start.2 = (bf16[8,2,32,384]{3,2,1,0:T(8,128)(2,1)S(1)}, bf16[8,2,32,384]{3,2,1,0:T(8,128)(2,1)S(1)}, u32[]{:S(2)}, u32[]{:S(2)}) collective-permute-start(bf16[8,2,32,384]{3,2,1,0:T(8,128)(2,1)S(1)} %slice.7.own_ref), channel_id=1, source_target_pairs={{0,8},{8,0},{16,24},{24,16},{32,40},{40,32},{48,56},{56,48},{64,72... | collective-permute-start | bytes 1179656 | tf_op jit(solution)/shard_map/ppermute | solution.py:215
  33.5 0.7 copy-start.2
  43.7 2.7 %copy-start.4 = (bf16[8,2,32,384]{3,2,1,0:T(8,128)(2,1)}, bf16[8,2,32,384]{3,2,1,0:T(8,128)(2,1)S(1)}, u32[]{:S(2)}) copy-start(bf16[8,2,32,384]{3,2,1,0:T(8,128)(2,1)S(1)} %collective-permute-done.1.ahead_ref) | copy-start | bytes 1179652
  43.8 10.6 %collective-permute-start.3 = (bf16[8,2,32,384]{3,2,1,0:T(8,128)(2,1)S(1)}, bf16[8,2,32,384]{3,2,1,0:T(8,128)(2,1)S(1)}, u32[]{:S(2)}, u32[]{:S(2)}) collective-permute-start(bf16[8,2,32,384]{3,2,1,0:T(8,128)(2,1)S(1)} %broadcast_select_fusion), channel_id=1, source_target_pairs={{0,248},{8,16},{16,8},{24,32},{32,24},{40,48},{48,40},{56,64},{64,... | collective-permute-start | bytes 1179656 | tf_op jit(solution)/shard_map/ppermute | solution.py:215
  45.9 8.5 %collective-permute-start.4 = (bf16[8,2,32,384]{3,2,1,0:T(8,128)(2,1)S(1)}, bf16[8,2,32,384]{3,2,1,0:T(8,128)(2,1)S(1)}, u32[]{:S(2)}, u32[]{:S(2)}) collective-permute-start(bf16[8,2,32,384]{3,2,1,0:T(8,128)(2,1)S(1)} %collective-permute-done.behind_ref), channel_id=1, source_target_pairs={{0,8},{8,0},{16,24},{24,16},{32,40},{40,32},{48,56},{56,48},{64,72... | collective-permute-start | bytes 1179656 | tf_op jit(solution)/shard_map/ppermute | solution.py:215
  45.9 8.5 %collective-permute-start.5 = (bf16[8,2,32,384]{3,2,1,0:T(8,128)(2,1)S(1)}, bf16[8,2,32,384]{3,2,1,0:T(8,128)(2,1)S(1)}, u32[]{:S(2)}, u32[]{:S(2)}) collective-permute-start(bf16[8,2,32,384]{3,2,1,0:T(8,128)(2,1)S(1)} %collective-permute-done.1.ahead_ref), channel_id=1, source_target_pairs={{0,8},{8,0},{16,24},{24,16},{32,40},{40,32},{48,56},{56,48},{64,72... | collective-permute-start | bytes 1179656 | tf_op jit(solution)/shard_map/ppermute | solution.py:215

commit v4 on v3

--- a/solution.py
+++ b/solution.py
@@ -16,7 +16,7 @@
 SCALE = math.log2(math.e) / math.sqrt(HD)
 GROUP = 6
 FIRST = 24
-VMEM_BYTES = 50 * 1024 * 1024
+VMEM_BYTES = 48 * 1024 * 1024
 
 
 def columns(head):
@@ -98,31 +98,40 @@
     return jnp.where(me % 2 == 0, 1, -1)
 
 
-def order_kernel(me_ref, plan_ref, refresh_ref, order_ref):
-    own = plan_ref[me_ref[0]]
+def order_kernel(me_ref, plan_ref, refresh_ref, cache_ref, order_ref, early, arrived):
+    one = jnp.int32(1)
+    fresh = jnp.left_shift(one, plan_ref[me_ref[0]])
+    for slot in range(SLOTS):
+        patch = refresh_ref[0, slot]
+        fresh = fresh | jnp.where(patch >= 0, jnp.left_shift(one, jnp.maximum(patch, 0)), 0)
     count = jnp.int32(0)
     for patch in range(PATCHES):
         order_ref[count] = jnp.int32(patch)
-        fresh = jnp.logical_or(own == patch, listing(patch, refresh_ref))
-        count = count + jnp.where(fresh, 0, 1)
+        count = count + 1 - (jnp.right_shift(fresh, patch) & 1)
     order_ref[PATCHES] = count
-
-
-def first_kernel(order_ref, cache_ref, query_ref, top_ref, sum_ref, acc_ref, held, arrived):
+    copies = [fetch(order_ref[place], place, cache_ref, early, arrived) for place in range(GROUP)]
+    for copy in copies:
+        copy.start()
+    for copy in copies:
+        copy.wait()
+
+
+def first_kernel(order_ref, cache_ref, query_ref, early, top_ref, sum_ref, acc_ref, held, arrived):
     def begin(group):
         for place in range(GROUP):
             place = group * GROUP + place
-            fetch(order_ref[place], place, cache_ref, held, arrived).start()
+            fetch(order_ref[GROUP + place], place, cache_ref, held, arrived).start()
 
     begin(0)
     begin(1)
     state = (top_ref, sum_ref, acc_ref)
     for target, value in zip(state, (-jnp.inf, 0.0, 0.0)):
         target[...] = jnp.full(target.shape, value, jnp.float32)
-
-    @pl.loop(0, FIRST // GROUP)
+    attend(query_ref, [cached(early, place) for place in range(GROUP)], [None] * GROUP, state)
+
+    @pl.loop(0, FIRST // GROUP - 1)
     def _(group):
-        @pl.when(group + 2 < FIRST // GROUP)
+        @pl.when(group + 2 < FIRST // GROUP - 1)
         def _():
             begin(group + 2)
 
@@ -201,13 +210,17 @@
     )(*scalars, *cache, *arrays)
 
 
-def stale_order(scalars):
+def stale_order(scalars, cache):
     return pl.pallas_call(
         order_kernel,
-        out_shape=jax.ShapeDtypeStruct((PATCHES + 1,), jnp.int32),
-        in_specs=[SMEM_SPEC] * 3,
-        out_specs=SMEM_SPEC,
-    )(*scalars)
+        out_shape=(
+            jax.ShapeDtypeStruct((PATCHES + 1,), jnp.int32), jax.ShapeDtypeStruct((2, GROUP, PT, WIDE), cache.dtype)
+        ),
+        in_specs=[SMEM_SPEC] * 3 + [pl.BlockSpec(memory_space=pl.ANY)],
+        out_specs=(SMEM_SPEC, VMEM_SPEC),
+        scratch_shapes=[pltpu.SemaphoreType.DMA((GROUP,))],
+        compiler_params=pltpu.CompilerParams(vmem_limit_bytes=VMEM_BYTES),
+    )(*scalars, cache)
 
 
 def move(value, target):
@@ -227,14 +240,14 @@
     outgoing = fresh_qkv.reshape(rows, 3, devices, WIDE).transpose(2, 1, 0, 3)
     heads = exchange(outgoing)
     cache = stale_cache[0].transpose(1, 0, 2)
-    order = stale_order(scalars)
-    heads, cache, order = lax.optimization_barrier((heads, cache, order))
+    order, early = stale_order(scalars, cache)
+    heads, cache, order, early = lax.optimization_barrier((heads, cache, order, early))
     own, query = heads[:, 1:3], heads[:, 0]
     twin = lambda s: s ^ 1
     behind = move(own, lambda s: s + 2)
     ahead = move(own, lambda s: s - 2)
     beside = move(own, twin)
-    state = run(first_kernel, FIRST, (order,), (query,), STATE, patches(FIRST), (cache,))
+    state = run(first_kernel, FIRST, (order,), (query, early), STATE, patches(FIRST - GROUP), (cache,))
     state, behind, ahead = lax.optimization_barrier((state, behind, ahead))
     beside_behind = move(behind, twin)
     beside_ahead = move(ahead, twin)

time: 69.4 us -> 68.5 us (0.987)
  waiting for transfers between devices: 8.85 us -> 7.16 us
  Pallas kernels: 16.3 us -> 17.6 us
    all_to_all x1, waiting for transfers between devices: 4.41 us -> 2.91 us  [exchange(): return lax.all_to_all(value, 'uly', split_axis=0, concat_axis=0, tiled=True)]
    pallas_call x1, Pallas kernels: 1.48 us -> 2.87 us  [stale_order(): pl.pallas_call(order_kernel, out_shape=(jax.ShapeDtypeStruct((PATCHES + 1...]
    unnamed x11 -> x5, local copies, waits for them, and re-layouts: 12.2 us -> 11.7 us
  transfers between devices with their start and end apart: 7 -> 7, of which waited for: 2 -> 2; matrix products, arithmetic and copies ran while one was open for 17% -> 17% of each run, Pallas kernels for 21% -> 23%
where the time goes in v4:
time: 68.5 us; the launch traced here: 68.2 us
  Pallas kernels  17.6 us (26%)
  starting transfers between devices  16.6 us (24%)
  local copies, waits for them, and re-layouts  14.4 us (21%)
  blocking collectives  12.3 us (18%)
  waiting for transfers between devices  7.16 us (10%)
    pallas_call x3, Pallas kernels, run(): pl.pallas_call(kernel, out_shape=out_shape, in_specs=[SMEM_SPEC] * len(sc...  14.8 us
    all_to_all x1, blocking collectives, exchange(): return lax.all_to_all(value, 'uly', split_axis=0, concat_axis=0, tiled=True)  12.3 us
    unnamed x5, local copies, waits for them, and re-layouts  11.7 us
    all_to_all x1, starting transfers between devices, exchange(): return lax.all_to_all(value, 'uly', split_axis=0, concat_axis=0, tiled=True)  8.57 us
    ppermute x6, starting transfers between devices, move(): lax.ppermute(value, 'pipe', [(source, target(source) % count) for source...  8.02 us
    ppermute x6, waiting for transfers between devices, move(): lax.ppermute(value, 'pipe', [(source, target(source) % count) for source...  4.25 us
    all_to_all x1, waiting for transfers between devices, exchange(): return lax.all_to_all(value, 'uly', split_axis=0, concat_axis=0, tiled=True)  2.91 us
    pallas_call x1, Pallas kernels, stale_order(): pl.pallas_call(order_kernel, out_shape=(jax.ShapeDtypeStruct((PATCHES + 1...  2.87 us
  transfers between devices with their start and end apart: 7, of which 2 were waited for; matrix products, arithmetic and copies ran while one was open for 17% of the time, Pallas kernels for 23%

profile of v4, /device:TPU:32, one launch (start us, length us, event | category | flops | bytes accessed | tf_op | source)
XLA Modules:
  0.0 68.2 jit_solution(6106743204400501029)
XLA Ops:
  0.0 2.0 %copy.14 = bf16[3,4,8,8,384]{4,3,1,0,2:T(8,128)(2,1)} copy(bf16[3,4,8,8,384]{4,3,2,1,0:T(8,128)(2,1)} %bitcast.22) | data formatting | bytes 1179648 | tf_op jit(solution)/shard_map/reshape | solution.py:240
  2.0 8.6 %all-to-all-start = ((bf16[8,3,32,384]{3,2,1,0:T(8,128)(2,1)}), bf16[8,3,32,384]{3,2,1,0:T(8,128)(2,1)S(1)}, u32[]{:S(2)}, u32[]{:S(2)}) async-start(bf16[8,3,32,384]{3,2,1,0:T(8,128)(2,1)} %bitcast.17), calls=%async_computation | async-start | bytes 1179648 | tf_op jit(solution)/shard_map/all_to_all | solution.py:232
  10.6 0.0 copy-start
  10.6 0.0 copy-start.1
  10.6 11.6 %copy.13 = bf16[1,8192,2,384]{3,1,2,0:T(8,128)(2,1)} copy(bf16[1,8192,2,384]{3,2,1,0:T(2,128)(2,1)} %param.5) | data formatting | bytes 25165824 | tf_op args[1]
  22.2 0.0 copy-done
  22.2 0.0 copy-done.1
  22.2 2.9 %shard_map.46 = (s32[33]{0:T(128)S(1)}, bf16[2,6,256,384]{3,2,1,0:T(8,128)(2,1)S(1)}) custom-call(s32[1]{0:T(128)} %bitcast.me_ref, s32[32]{0:T(128)S(1)} %copy-done, s32[1,6]{1,0:T(1,128)S(1)} %copy-done.1, bf16[2,8192,384]{2,1,0:T(8,128)(2,1)} %bitcast.18), custom_call_target="tpu_custom_call" | custom-call | tf_op jit(solution)/shard_map/pallas_call | solution.py:214
  25.1 2.9 %all-to-all-done = bf16[8,3,32,384]{3,2,1,0:T(8,128)(2,1)S(1)} async-done(((bf16[8,3,32,384]{3,2,1,0:T(8,128)(2,1)}), bf16[8,3,32,384]{3,2,1,0:T(8,128)(2,1)S(1)}, u32[]{:S(2)}, u32[]{:S(2)}) %all-to-all-start) | async-done | bytes 589856 | tf_op jit(solution)/shard_map/all_to_all | solution.py:232
  28.1 1.7 %collective-permute-start = (bf16[8,2,32,384]{3,2,1,0:T(8,128)(2,1)S(1)}, bf16[8,2,32,384]{3,2,1,0:T(8,128)(2,1)S(1)}, u32[]{:S(2)}, u32[]{:S(2)}) collective-permute-start(bf16[8,2,32,384]{3,2,1,0:T(8,128)(2,1)S(1)} %slice.7.own_ref), channel_id=1, source_target_pairs={{0,16},{8,24},{16,32},{24,40},{32,48},{40,56},{48,64},{56,72},{64,... | collective-permute-start | bytes 1179656 | tf_op jit(solution)/shard_map/ppermute | solution.py:228
  29.7 3.8 %collective-permute-start.1 = (bf16[8,2,32,384]{3,2,1,0:T(8,128)(2,1)S(1)}, bf16[8,2,32,384]{3,2,1,0:T(8,128)(2,1)S(1)}, u32[]{:S(2)}, u32[]{:S(2)}) collective-permute-start(bf16[8,2,32,384]{3,2,1,0:T(8,128)(2,1)S(1)} %slice.7.own_ref), channel_id=1, source_target_pairs={{0,240},{8,248},{16,0},{24,8},{32,16},{40,24},{48,32},{56,40},{64,... | collective-permute-start | bytes 1179656 | tf_op jit(solution)/shard_map/ppermute | solution.py:228
  33.5 0.0 collective-permute-start.2
  33.5 9.2 %shard_map.47 = (f32[3,256,128]{2,1,0:T(8,128)S(1)}, f32[3,256,128]{2,1,0:T(8,128)S(1)}, f32[3,256,128]{2,1,0:T(8,128)S(1)}) custom-call(s32[33]{0:T(128)S(1)} %get-tuple-element.25.order_ref, bf16[2,8192,384]{2,1,0:T(8,128)(2,1)} %bitcast.19, bf16[8,32,384]{2,1,0:T(8,128)(2,1)S(1)} %slice_bitcast_fusion.query_ref, ...), custom_call_target="tpu_custom_call" | custom-call | flops 4831838208 | bytes 9437184 | tf_op jit(solution)/shard_map/pallas_call | solution.py:200
  42.7 0.0 collective-permute-done.behind_ref
  42.7 0.0 collective-permute-done.1.ahead_ref
  42.7 0.1 broadcast_select_fusion
  42.8 2.1 %collective-permute-start.3 = (bf16[8,2,32,384]{3,2,1,0:T(8,128)(2,1)S(1)}, bf16[8,2,32,384]{3,2,1,0:T(8,128)(2,1)S(1)}, u32[]{:S(2)}, u32[]{:S(2)}) collective-permute-start(bf16[8,2,32,384]{3,2,1,0:T(8,128)(2,1)S(1)} %broadcast_select_fusion), channel_id=1, source_target_pairs={{0,248},{8,16},{16,8},{24,32},{32,24},{40,48},{48,40},{56,64},{64,... | collective-permute-start | bytes 1179656 | tf_op jit(solution)/shard_map/ppermute | solution.py:228
  44.9 0.0 collective-permute-start.4
  44.9 0.5 collective-permute-start.5
  45.4 0.0 collective-permute-done.2.beside_ref
  45.4 3.8 %shard_map.48 = (f32[3,256,128]{2,1,0:T(8,128)S(1)}, f32[3,256,128]{2,1,0:T(8,128)S(1)}, f32[3,256,128]{2,1,0:T(8,128)S(1)}) custom-call(s32[1]{0:T(128)} %bitcast.me_ref, s32[32]{0:T(128)S(1)} %copy-done, s32[1,6]{1,0:T(1,128)S(1)} %copy-done.1, s32[33]{0:T(128)S(1)} %get-tuple-element.25.order_ref, bf16[2,8192,384]{2,1,0:T(8,128)(2,1)} %bitcast.20, ...), custom_call_target="tpu_custom_call" | custom-call | flops 1610612736 | bytes 3145728 | tf_op jit(solution)/shard_map/pallas_call | solution.py:200
  49.2 4.2 %collective-permute-done.3.far_ref = bf16[8,2,32,384]{3,2,1,0:T(8,128)(2,1)S(1)} collective-permute-done((bf16[8,2,32,384]{3,2,1,0:T(8,128)(2,1)S(1)}, bf16[8,2,32,384]{3,2,1,0:T(8,128)(2,1)S(1)}, u32[]{:S(2)}, u32[]{:S(2)}) %collective-permute-start.3) | collective-permute-done | bytes 393248 | tf_op jit(solution)/shard_map/ppermute | solution.py:228
  53.4 0.0 collective-permute-done.4.beside_behind_ref
  53.4 0.0 collective-permute-done.5.beside_ahead_ref
  53.4 1.8 %shard_map.49 = bf16[8,32,384]{2,1,0:T(8,128)(2,1)S(1)} custom-call(s32[1]{0:T(128)} %bitcast.me_ref, s32[32]{0:T(128)S(1)} %copy-done, s32[1,6]{1,0:T(1,128)S(1)} %copy-done.1, bf16[8,32,384]{2,1,0:T(8,128)(2,1)S(1)} %slice_bitcast_fusion.query_ref, f32[3,256,128]{2,1,0:T(8,128)S(1)} %get-tuple-element.36.top_in, ...), custom_call_target="tpu_custom_call" | custom-call | flops 603979776 | bytes 1179648 | tf_op jit(solution)/shard_map/pallas_call | solution.py:200
  55.2 12.3 %all_to_all.10 = bf16[8,32,384]{2,1,0:T(8,128)(2,1)S(1)} all-to-all(bf16[8,32,384]{2,1,0:T(8,128)(2,1)S(1)} %shard_map.49), channel_id=1, replica_groups=mesh['pipe'=32,'uly'=8] {'uly'}, dimensions={0} | all-to-all | bytes 393216 | tf_op jit(solution)/shard_map/all_to_all | solution.py:232
  67.5 0.7 %copy.10 = bf16[8,4,8,384]{3,2,0,1:T(8,128)(2,1)} copy(bf16[8,4,8,384]{3,2,1,0:T(8,128)(2,1)S(1)} %bitcast.21) | data formatting | bytes 393216 | tf_op jit(solution)/shard_map/reshape | solution.py:265
  (2 shorter events, 0.1 us)
Async XLA Ops:
  2.0 26.0 %all-to-all-start = ((bf16[8,3,32,384]{3,2,1,0:T(8,128)(2,1)}), bf16[8,3,32,384]{3,2,1,0:T(8,128)(2,1)S(1)}, u32[]{:S(2)}, u32[]{:S(2)}) async-start(bf16[8,3,32,384]{3,2,1,0:T(8,128)(2,1)} %bitcast.17), calls=%async_computation | async-start | bytes 1179648 | tf_op jit(solution)/shard_map/all_to_all | solution.py:232
  10.6 11.7 %copy-start = (s32[32]{0:T(128)S(1)}, s32[32]{0:T(128)}, u32[]{:S(2)}) copy-start(s32[32]{0:T(128)} %plan_ref.5) | copy-start | bytes 388
  10.6 11.7 %copy-start.1 = (s32[1,6]{1,0:T(1,128)S(1)}, s32[1,6]{1,0:T(1,128)}, u32[]{:S(2)}) copy-start(s32[1,6]{1,0:T(1,128)} %refresh_ref.5) | copy-start | bytes 76
  28.1 14.6 %collective-permute-start = (bf16[8,2,32,384]{3,2,1,0:T(8,128)(2,1)S(1)}, bf16[8,2,32,384]{3,2,1,0:T(8,128)(2,1)S(1)}, u32[]{:S(2)}, u32[]{:S(2)}) collective-permute-start(bf16[8,2,32,384]{3,2,1,0:T(8,128)(2,1)S(1)} %slice.7.own_ref), channel_id=1, source_target_pairs={{0,16},{8,24},{16,32},{24,40},{32,48},{40,56},{48,64},{56,72},{64,... | collective-permute-start | bytes 1179656 | tf_op jit(solution)/shard_map/ppermute | solution.py:228
  29.7 13.0 %collective-permute-start.1 = (bf16[8,2,32,384]{3,2,1,0:T(8,128)(2,1)S(1)}, bf16[8,2,32,384]{3,2,1,0:T(8,128)(2,1)S(1)}, u32[]{:S(2)}, u32[]{:S(2)}) collective-permute-start(bf16[8,2,32,384]{3,2,1,0:T(8,128)(2,1)S(1)} %slice.7.own_ref), channel_id=1, source_target_pairs={{0,240},{8,248},{16,0},{24,8},{32,16},{40,24},{48,32},{56,40},{64,... | collective-permute-start | bytes 1179656 | tf_op jit(solution)/shard_map/ppermute | solution.py:228
  33.5 11.9 %collective-permute-start.2 = (bf16[8,2,32,384]{3,2,1,0:T(8,128)(2,1)S(1)}, bf16[8,2,32,384]{3,2,1,0:T(8,128)(2,1)S(1)}, u32[]{:S(2)}, u32[]{:S(2)}) collective-permute-start(bf16[8,2,32,384]{3,2,1,0:T(8,128)(2,1)S(1)} %slice.7.own_ref), channel_id=1, source_target_pairs={{0,8},{8,0},{16,24},{24,16},{32,40},{40,32},{48,56},{56,48},{64,72... | collective-permute-start | bytes 1179656 | tf_op jit(solution)/shard_map/ppermute | solution.py:228
  42.8 10.6 %collective-permute-start.3 = (bf16[8,2,32,384]{3,2,1,0:T(8,128)(2,1)S(1)}, bf16[8,2,32,384]{3,2,1,0:T(8,128)(2,1)S(1)}, u32[]{:S(2)}, u32[]{:S(2)}) collective-permute-start(bf16[8,2,32,384]{3,2,1,0:T(8,128)(2,1)S(1)} %broadcast_select_fusion), channel_id=1, source_target_pairs={{0,248},{8,16},{16,8},{24,32},{32,24},{40,48},{48,40},{56,64},{64,... | collective-permute-start | bytes 1179656 | tf_op jit(solution)/shard_map/ppermute | solution.py:228
  44.9 8.5 %collective-permute-start.4 = (bf16[8,2,32,384]{3,2,1,0:T(8,128)(2,1)S(1)}, bf16[8,2,32,384]{3,2,1,0:T(8,128)(2,1)S(1)}, u32[]{:S(2)}, u32[]{:S(2)}) collective-permute-start(bf16[8,2,32,384]{3,2,1,0:T(8,128)(2,1)S(1)} %collective-permute-done.behind_ref), channel_id=1, source_target_pairs={{0,8},{8,0},{16,24},{24,16},{32,40},{40,32},{48,56},{56,48},{64,72... | collective-permute-start | bytes 1179656 | tf_op jit(solution)/shard_map/ppermute | solution.py:228
  44.9 8.5 %collective-permute-start.5 = (bf16[8,2,32,384]{3,2,1,0:T(8,128)(2,1)S(1)}, bf16[8,2,32,384]{3,2,1,0:T(8,128)(2,1)S(1)}, u32[]{:S(2)}, u32[]{:S(2)}) collective-permute-start(bf16[8,2,32,384]{3,2,1,0:T(8,128)(2,1)S(1)} %collective-permute-done.1.ahead_ref), channel_id=1, source_target_pairs={{0,8},{8,0},{16,24},{24,16},{32,40},{40,32},{48,56},{56,48},{64,72... | collective-permute-start | bytes 1179656 | tf_op jit(solution)/shard_map/ppermute | solution.py:228

commit v5 on v4

--- a/solution.py
+++ b/solution.py
@@ -45,12 +45,10 @@
             parts.append(probs.astype(jnp.bfloat16))
         weights = jnp.concatenate(parts, axis=1)
         mixed = mixed + jnp.dot(weights, value, preferred_element_type=jnp.float32)
-    acc_ref[head] = mixed
-    sum_ref[head] = total
-    top_ref[head] = top
-
-
-def attend(query_ref, readers, biases, state):
+    return top, total, mixed
+
+
+def absorbed(query_ref, readers, biases, source):
     scores = []
     for head in range(LOCAL):
         query = query_ref[:, :, columns(head)].reshape(PT, HD)
@@ -59,7 +57,15 @@
             for read in readers
         ])
     for head in range(LOCAL):
-        absorb(head, scores[head], [read(1, head) for read in readers], biases, *state)
+        yield head, absorb(head, scores[head], [read(1, head) for read in readers], biases, *source)
+
+
+def attend(query_ref, readers, biases, state, source=None):
+    top_ref, sum_ref, acc_ref = state
+    for head, (top, total, mixed) in absorbed(query_ref, readers, biases, source or state):
+        acc_ref[head] = mixed
+        sum_ref[head] = total
+        top_ref[head] = top
 
 
 def cached(held, place):
@@ -147,14 +153,12 @@
         fetch(order_ref[FIRST + place], place, cache_ref, held, arrived).start()
 
     state = (top_ref, sum_ref, acc_ref)
-    for source, target in zip((top_in, sum_in, acc_in), state):
-        target[...] = source[...]
     me = me_ref[0]
     biases = [None] + [
         bias_of(section, plan_ref, refresh_ref) for section in (me + sign_of(me), me - 2, me + 2)
     ]
     readers = [moved(block) for block in (own_ref, beside_ref, behind_ref, ahead_ref)]
-    attend(query_ref, readers, biases, state)
+    attend(query_ref, readers, biases, state, (top_in, sum_in, acc_in))
 
     @pl.when(left >= 4)
     def _():
@@ -169,20 +173,15 @@
 
 
 def last_kernel(me_ref, plan_ref, refresh_ref, query_ref, top_in, sum_in, acc_in, far_ref, beside_behind_ref,
-                beside_ahead_ref, out_ref, top_ref, sum_ref, acc_ref):
-    state = (top_ref, sum_ref, acc_ref)
-    for source, target in zip((top_in, sum_in, acc_in), state):
-        target[...] = source[...]
+                beside_ahead_ref, out_ref):
     me = me_ref[0]
     sign = sign_of(me)
     biases = [
         bias_of(section, plan_ref, refresh_ref) for section in (me - 3 * sign, me + sign - 2, me + sign + 2)
     ]
     readers = [moved(block) for block in (far_ref, beside_behind_ref, beside_ahead_ref)]
-    attend(query_ref, readers, biases, state)
-    for head in range(LOCAL):
-        total = jnp.sum(sum_ref[head], axis=1, keepdims=True)
-        done = (acc_ref[head] / total).astype(jnp.bfloat16)
+    for head, (_, total, mixed) in absorbed(query_ref, readers, biases, (top_in, sum_in, acc_in)):
+        done = (mixed / jnp.sum(total, axis=1, keepdims=True)).astype(jnp.bfloat16)
         out_ref[:, :, columns(head)] = done.reshape(out_ref.shape[0], out_ref.shape[1], HD)
 
 
@@ -256,10 +255,9 @@
         second_kernel, 8, (*scalars, order), (query, *state, own, beside, behind, ahead), STATE,
         patches(PATCHES - 1 - FIRST), (cache,),
     )
-    held = pltpu.VMEM((LOCAL, PT, HD), jnp.float32)
     mixed = run(
         last_kernel, 3, scalars, (query, *state, far, beside_behind, beside_ahead),
-        jax.ShapeDtypeStruct(query.shape, jnp.bfloat16), [held] * 3,
+        jax.ShapeDtypeStruct(query.shape, jnp.bfloat16), [],
     )
     back = exchange(mixed)
     return back.transpose(1, 0, 2).reshape(rows, devices * WIDE)

time: 68.5 us -> 68.5 us (level)
  no operation moved by 1% of the time
where the time goes in v5:
time: 68.5 us; the launch traced here: 68.2 us
  Pallas kernels  17.6 us (26%)
  starting transfers between devices  16.6 us (24%)
  local copies, waits for them, and re-layouts  14.4 us (21%)
  blocking collectives  12.3 us (18%)
  waiting for transfers between devices  7.16 us (10%)
    pallas_call x3, Pallas kernels, run(): pl.pallas_call(kernel, out_shape=out_shape, in_specs=[SMEM_SPEC] * len(sc...  14.8 us
    all_to_all x1, blocking collectives, exchange(): return lax.all_to_all(value, 'uly', split_axis=0, concat_axis=0, tiled=True)  12.3 us
    unnamed x5, local copies, waits for them, and re-layouts  11.7 us
    all_to_all x1, starting transfers between devices, exchange(): return lax.all_to_all(value, 'uly', split_axis=0, concat_axis=0, tiled=True)  8.57 us
    ppermute x6, starting transfers between devices, move(): lax.ppermute(value, 'pipe', [(source, target(source) % count) for source...  8.02 us
    ppermute x6, waiting for transfers between devices, move(): lax.ppermute(value, 'pipe', [(source, target(source) % count) for source...  4.25 us
    all_to_all x1, waiting for transfers between devices, exchange(): return lax.all_to_all(value, 'uly', split_axis=0, concat_axis=0, tiled=True)  2.91 us
    pallas_call x1, Pallas kernels, stale_order(): pl.pallas_call(order_kernel, out_shape=(jax.ShapeDtypeStruct((PATCHES + 1...  2.87 us
  transfers between devices with their start and end apart: 7, of which 2 were waited for; matrix products, arithmetic and copies ran while one was open for 17% of the time, Pallas kernels for 23%

profile of v5, /device:TPU:32, one launch (start us, length us, event | category | flops | bytes accessed | tf_op | source)
XLA Modules:
  0.0 68.2 jit_solution(4253585903274604659)
XLA Ops:
  0.0 2.0 %copy.14 = bf16[3,4,8,8,384]{4,3,1,0,2:T(8,128)(2,1)} copy(bf16[3,4,8,8,384]{4,3,2,1,0:T(8,128)(2,1)} %bitcast.22) | data formatting | bytes 1179648 | tf_op jit(solution)/shard_map/reshape | solution.py:239
  2.0 8.6 %all-to-all-start = ((bf16[8,3,32,384]{3,2,1,0:T(8,128)(2,1)}), bf16[8,3,32,384]{3,2,1,0:T(8,128)(2,1)S(1)}, u32[]{:S(2)}, u32[]{:S(2)}) async-start(bf16[8,3,32,384]{3,2,1,0:T(8,128)(2,1)} %bitcast.17), calls=%async_computation | async-start | bytes 1179648 | tf_op jit(solution)/shard_map/all_to_all | solution.py:231
  10.6 0.0 copy-start
  10.6 0.0 copy-start.1
  10.6 11.6 %copy.13 = bf16[1,8192,2,384]{3,1,2,0:T(8,128)(2,1)} copy(bf16[1,8192,2,384]{3,2,1,0:T(2,128)(2,1)} %param.5) | data formatting | bytes 25165824 | tf_op args[1]
  22.2 0.0 copy-done
  22.2 0.0 copy-done.1
  22.2 2.9 %shard_map.46 = (s32[33]{0:T(128)S(1)}, bf16[2,6,256,384]{3,2,1,0:T(8,128)(2,1)S(1)}) custom-call(s32[1]{0:T(128)} %bitcast.me_ref, s32[32]{0:T(128)S(1)} %copy-done, s32[1,6]{1,0:T(1,128)S(1)} %copy-done.1, bf16[2,8192,384]{2,1,0:T(8,128)(2,1)} %bitcast.18), custom_call_target="tpu_custom_call" | custom-call | tf_op jit(solution)/shard_map/pallas_call | solution.py:213
  25.1 2.9 %all-to-all-done = bf16[8,3,32,384]{3,2,1,0:T(8,128)(2,1)S(1)} async-done(((bf16[8,3,32,384]{3,2,1,0:T(8,128)(2,1)}), bf16[8,3,32,384]{3,2,1,0:T(8,128)(2,1)S(1)}, u32[]{:S(2)}, u32[]{:S(2)}) %all-to-all-start) | async-done | bytes 589856 | tf_op jit(solution)/shard_map/all_to_all | solution.py:231
  28.1 1.7 %collective-permute-start = (bf16[8,2,32,384]{3,2,1,0:T(8,128)(2,1)S(1)}, bf16[8,2,32,384]{3,2,1,0:T(8,128)(2,1)S(1)}, u32[]{:S(2)}, u32[]{:S(2)}) collective-permute-start(bf16[8,2,32,384]{3,2,1,0:T(8,128)(2,1)S(1)} %slice.7.own_ref), channel_id=1, source_target_pairs={{0,16},{8,24},{16,32},{24,40},{32,48},{40,56},{48,64},{56,72},{64,... | collective-permute-start | bytes 1179656 | tf_op jit(solution)/shard_map/ppermute | solution.py:227
  29.7 3.8 %collective-permute-start.1 = (bf16[8,2,32,384]{3,2,1,0:T(8,128)(2,1)S(1)}, bf16[8,2,32,384]{3,2,1,0:T(8,128)(2,1)S(1)}, u32[]{:S(2)}, u32[]{:S(2)}) collective-permute-start(bf16[8,2,32,384]{3,2,1,0:T(8,128)(2,1)S(1)} %slice.7.own_ref), channel_id=1, source_target_pairs={{0,240},{8,248},{16,0},{24,8},{32,16},{40,24},{48,32},{56,40},{64,... | collective-permute-start | bytes 1179656 | tf_op jit(solution)/shard_map/ppermute | solution.py:227
  33.5 0.0 collective-permute-start.2
  33.5 9.2 %shard_map.47 = (f32[3,256,128]{2,1,0:T(8,128)S(1)}, f32[3,256,128]{2,1,0:T(8,128)S(1)}, f32[3,256,128]{2,1,0:T(8,128)S(1)}) custom-call(s32[33]{0:T(128)S(1)} %get-tuple-element.25.order_ref, bf16[2,8192,384]{2,1,0:T(8,128)(2,1)} %bitcast.19, bf16[8,32,384]{2,1,0:T(8,128)(2,1)S(1)} %slice_bitcast_fusion.query_ref, ...), custom_call_target="tpu_custom_call" | custom-call | flops 4831838208 | bytes 9437184 | tf_op jit(solution)/shard_map/pallas_call | solution.py:199
  42.7 0.0 collective-permute-done.behind_ref
  42.7 0.0 collective-permute-done.1.ahead_ref
  42.7 0.1 broadcast_select_fusion
  42.8 2.1 %collective-permute-start.3 = (bf16[8,2,32,384]{3,2,1,0:T(8,128)(2,1)S(1)}, bf16[8,2,32,384]{3,2,1,0:T(8,128)(2,1)S(1)}, u32[]{:S(2)}, u32[]{:S(2)}) collective-permute-start(bf16[8,2,32,384]{3,2,1,0:T(8,128)(2,1)S(1)} %broadcast_select_fusion), channel_id=1, source_target_pairs={{0,248},{8,16},{16,8},{24,32},{32,24},{40,48},{48,40},{56,64},{64,... | collective-permute-start | bytes 1179656 | tf_op jit(solution)/shard_map/ppermute | solution.py:227
  44.9 0.0 collective-permute-start.4
  44.9 0.5 collective-permute-start.5
  45.4 0.0 collective-permute-done.2.beside_ref
  45.4 3.8 %shard_map.48 = (f32[3,256,128]{2,1,0:T(8,128)S(1)}, f32[3,256,128]{2,1,0:T(8,128)S(1)}, f32[3,256,128]{2,1,0:T(8,128)S(1)}) custom-call(s32[1]{0:T(128)} %bitcast.me_ref, s32[32]{0:T(128)S(1)} %copy-done, s32[1,6]{1,0:T(1,128)S(1)} %copy-done.1, s32[33]{0:T(128)S(1)} %get-tuple-element.25.order_ref, bf16[2,8192,384]{2,1,0:T(8,128)(2,1)} %bitcast.20, ...), custom_call_target="tpu_custom_call" | custom-call | flops 1610612736 | bytes 3145728 | tf_op jit(solution)/shard_map/pallas_call | solution.py:199
  49.2 4.2 %collective-permute-done.3.far_ref = bf16[8,2,32,384]{3,2,1,0:T(8,128)(2,1)S(1)} collective-permute-done((bf16[8,2,32,384]{3,2,1,0:T(8,128)(2,1)S(1)}, bf16[8,2,32,384]{3,2,1,0:T(8,128)(2,1)S(1)}, u32[]{:S(2)}, u32[]{:S(2)}) %collective-permute-start.3) | collective-permute-done | bytes 393248 | tf_op jit(solution)/shard_map/ppermute | solution.py:227
  53.4 0.0 collective-permute-done.4.beside_behind_ref
  53.4 0.0 collective-permute-done.5.beside_ahead_ref
  53.4 1.8 %shard_map.49 = bf16[8,32,384]{2,1,0:T(8,128)(2,1)S(1)} custom-call(s32[1]{0:T(128)} %bitcast.me_ref, s32[32]{0:T(128)S(1)} %copy-done, s32[1,6]{1,0:T(1,128)S(1)} %copy-done.1, bf16[8,32,384]{2,1,0:T(8,128)(2,1)S(1)} %slice_bitcast_fusion.query_ref, f32[3,256,128]{2,1,0:T(8,128)S(1)} %get-tuple-element.36.top_in, ...), custom_call_target="tpu_custom_call" | custom-call | flops 603979776 | bytes 1179648 | tf_op jit(solution)/shard_map/pallas_call | solution.py:199
  55.2 12.3 %all_to_all.10 = bf16[8,32,384]{2,1,0:T(8,128)(2,1)S(1)} all-to-all(bf16[8,32,384]{2,1,0:T(8,128)(2,1)S(1)} %shard_map.49), channel_id=1, replica_groups=mesh['pipe'=32,'uly'=8] {'uly'}, dimensions={0} | all-to-all | bytes 393216 | tf_op jit(solution)/shard_map/all_to_all | solution.py:231
  67.5 0.7 %copy.10 = bf16[8,4,8,384]{3,2,0,1:T(8,128)(2,1)} copy(bf16[8,4,8,384]{3,2,1,0:T(8,128)(2,1)S(1)} %bitcast.21) | data formatting | bytes 393216 | tf_op jit(solution)/shard_map/reshape | solution.py:263
  (2 shorter events, 0.1 us)
Async XLA Ops:
  2.0 26.0 %all-to-all-start = ((bf16[8,3,32,384]{3,2,1,0:T(8,128)(2,1)}), bf16[8,3,32,384]{3,2,1,0:T(8,128)(2,1)S(1)}, u32[]{:S(2)}, u32[]{:S(2)}) async-start(bf16[8,3,32,384]{3,2,1,0:T(8,128)(2,1)} %bitcast.17), calls=%async_computation | async-start | bytes 1179648 | tf_op jit(solution)/shard_map/all_to_all | solution.py:231
  10.6 11.7 %copy-start = (s32[32]{0:T(128)S(1)}, s32[32]{0:T(128)}, u32[]{:S(2)}) copy-start(s32[32]{0:T(128)} %plan_ref.5) | copy-start | bytes 388
  10.6 11.7 %copy-start.1 = (s32[1,6]{1,0:T(1,128)S(1)}, s32[1,6]{1,0:T(1,128)}, u32[]{:S(2)}) copy-start(s32[1,6]{1,0:T(1,128)} %refresh_ref.5) | copy-start | bytes 76
  28.1 14.6 %collective-permute-start = (bf16[8,2,32,384]{3,2,1,0:T(8,128)(2,1)S(1)}, bf16[8,2,32,384]{3,2,1,0:T(8,128)(2,1)S(1)}, u32[]{:S(2)}, u32[]{:S(2)}) collective-permute-start(bf16[8,2,32,384]{3,2,1,0:T(8,128)(2,1)S(1)} %slice.7.own_ref), channel_id=1, source_target_pairs={{0,16},{8,24},{16,32},{24,40},{32,48},{40,56},{48,64},{56,72},{64,... | collective-permute-start | bytes 1179656 | tf_op jit(solution)/shard_map/ppermute | solution.py:227
  29.7 13.0 %collective-permute-start.1 = (bf16[8,2,32,384]{3,2,1,0:T(8,128)(2,1)S(1)}, bf16[8,2,32,384]{3,2,1,0:T(8,128)(2,1)S(1)}, u32[]{:S(2)}, u32[]{:S(2)}) collective-permute-start(bf16[8,2,32,384]{3,2,1,0:T(8,128)(2,1)S(1)} %slice.7.own_ref), channel_id=1, source_target_pairs={{0,240},{8,248},{16,0},{24,8},{32,16},{40,24},{48,32},{56,40},{64,... | collective-permute-start | bytes 1179656 | tf_op jit(solution)/shard_map/ppermute | solution.py:227
  33.5 11.9 %collective-permute-start.2 = (bf16[8,2,32,384]{3,2,1,0:T(8,128)(2,1)S(1)}, bf16[8,2,32,384]{3,2,1,0:T(8,128)(2,1)S(1)}, u32[]{:S(2)}, u32[]{:S(2)}) collective-permute-start(bf16[8,2,32,384]{3,2,1,0:T(8,128)(2,1)S(1)} %slice.7.own_ref), channel_id=1, source_target_pairs={{0,8},{8,0},{16,24},{24,16},{32,40},{40,32},{48,56},{56,48},{64,72... | collective-permute-start | bytes 1179656 | tf_op jit(solution)/shard_map/ppermute | solution.py:227
  42.8 10.6 %collective-permute-start.3 = (bf16[8,2,32,384]{3,2,1,0:T(8,128)(2,1)S(1)}, bf16[8,2,32,384]{3,2,1,0:T(8,128)(2,1)S(1)}, u32[]{:S(2)}, u32[]{:S(2)}) collective-permute-start(bf16[8,2,32,384]{3,2,1,0:T(8,128)(2,1)S(1)} %broadcast_select_fusion), channel_id=1, source_target_pairs={{0,248},{8,16},{16,8},{24,32},{32,24},{40,48},{48,40},{56,64},{64,... | collective-permute-start | bytes 1179656 | tf_op jit(solution)/shard_map/ppermute | solution.py:227
  44.9 8.5 %collective-permute-start.4 = (bf16[8,2,32,384]{3,2,1,0:T(8,128)(2,1)S(1)}, bf16[8,2,32,384]{3,2,1,0:T(8,128)(2,1)S(1)}, u32[]{:S(2)}, u32[]{:S(2)}) collective-permute-start(bf16[8,2,32,384]{3,2,1,0:T(8,128)(2,1)S(1)} %collective-permute-done.behind_ref), channel_id=1, source_target_pairs={{0,8},{8,0},{16,24},{24,16},{32,40},{40,32},{48,56},{56,48},{64,72... | collective-permute-start | bytes 1179656 | tf_op jit(solution)/shard_map/ppermute | solution.py:227
  44.9 8.5 %collective-permute-start.5 = (bf16[8,2,32,384]{3,2,1,0:T(8,128)(2,1)S(1)}, bf16[8,2,32,384]{3,2,1,0:T(8,128)(2,1)S(1)}, u32[]{:S(2)}, u32[]{:S(2)}) collective-permute-start(bf16[8,2,32,384]{3,2,1,0:T(8,128)(2,1)S(1)} %collective-permute-done.1.ahead_ref), channel_id=1, source_target_pairs={{0,8},{8,0},{16,24},{24,16},{32,40},{40,32},{48,56},{56,48},{64,72... | collective-permute-start | bytes 1179656 | tf_op jit(solution)/shard_map/ppermute | solution.py:227

commit v6 on v4

--- a/solution.py
+++ b/solution.py
@@ -122,8 +122,8 @@
             place = group * GROUP + place
             fetch(order_ref[GROUP + place], place, cache_ref, held, arrived).start()
 
-    begin(0)
-    begin(1)
+    for group in range(FIRST // GROUP - 1):
+        begin(group)
     state = (top_ref, sum_ref, acc_ref)
     for target, value in zip(state, (-jnp.inf, 0.0, 0.0)):
         target[...] = jnp.full(target.shape, value, jnp.float32)
@@ -131,10 +131,6 @@
 
     @pl.loop(0, FIRST // GROUP - 1)
     def _(group):
-        @pl.when(group + 2 < FIRST // GROUP - 1)
-        def _():
-            begin(group + 2)
-
         attend_stale(group * GROUP, GROUP, query_ref, cache_ref, held, arrived, state)
 
 

time: 68.5 us -> 68.9 us (level)
  no operation moved by 1% of the time
where the time goes in v6:
time: 68.9 us; the launch traced here: 68.5 us
  Pallas kernels  17.7 us (26%)
  starting transfers between devices  16.6 us (24%)
  local copies, waits for them, and re-layouts  14.4 us (21%)
  blocking collectives  12.3 us (18%)
  waiting for transfers between devices  7.43 us (11%)
    pallas_call x3, Pallas kernels, run(): pl.pallas_call(kernel, out_shape=out_shape, in_specs=[SMEM_SPEC] * len(sc...  14.8 us
    all_to_all x1, blocking collectives, exchange(): return lax.all_to_all(value, 'uly', split_axis=0, concat_axis=0, tiled=True)  12.3 us
    unnamed x5, local copies, waits for them, and re-layouts  11.7 us
    all_to_all x1, starting transfers between devices, exchange(): return lax.all_to_all(value, 'uly', split_axis=0, concat_axis=0, tiled=True)  8.57 us
    ppermute x6, starting transfers between devices, move(): lax.ppermute(value, 'pipe', [(source, target(source) % count) for source...  8.02 us
    ppermute x6, waiting for transfers between devices, move(): lax.ppermute(value, 'pipe', [(source, target(source) % count) for source...  4.5 us
    all_to_all x1, waiting for transfers between devices, exchange(): return lax.all_to_all(value, 'uly', split_axis=0, concat_axis=0, tiled=True)  2.92 us
    pallas_call x1, Pallas kernels, stale_order(): pl.pallas_call(order_kernel, out_shape=(jax.ShapeDtypeStruct((PATCHES + 1...  2.85 us
  transfers between devices with their start and end apart: 7, of which 2 were waited for; matrix products, arithmetic and copies ran while one was open for 17% of the time, Pallas kernels for 23%

profile of v6, /device:TPU:32, one launch (start us, length us, event | category | flops | bytes accessed | tf_op | source)
XLA Modules:
  0.0 68.5 jit_solution(8120856912455374192)
XLA Ops:
  0.0 2.0 %copy.14 = bf16[3,4,8,8,384]{4,3,1,0,2:T(8,128)(2,1)} copy(bf16[3,4,8,8,384]{4,3,2,1,0:T(8,128)(2,1)} %bitcast.22) | data formatting | bytes 1179648 | tf_op jit(solution)/shard_map/reshape | solution.py:236
  2.0 8.6 %all-to-all-start = ((bf16[8,3,32,384]{3,2,1,0:T(8,128)(2,1)}), bf16[8,3,32,384]{3,2,1,0:T(8,128)(2,1)S(1)}, u32[]{:S(2)}, u32[]{:S(2)}) async-start(bf16[8,3,32,384]{3,2,1,0:T(8,128)(2,1)} %bitcast.17), calls=%async_computation | async-start | bytes 1179648 | tf_op jit(solution)/shard_map/all_to_all | solution.py:228
  10.6 0.0 copy-start
  10.6 0.0 copy-start.1
  10.6 11.6 %copy.13 = bf16[1,8192,2,384]{3,1,2,0:T(8,128)(2,1)} copy(bf16[1,8192,2,384]{3,2,1,0:T(2,128)(2,1)} %param.5) | data formatting | bytes 25165824 | tf_op args[1]
  22.2 0.0 copy-done
  22.2 0.0 copy-done.1
  22.2 2.9 %shard_map.46 = (s32[33]{0:T(128)S(1)}, bf16[2,6,256,384]{3,2,1,0:T(8,128)(2,1)S(1)}) custom-call(s32[1]{0:T(128)} %bitcast.me_ref, s32[32]{0:T(128)S(1)} %copy-done, s32[1,6]{1,0:T(1,128)S(1)} %copy-done.1, bf16[2,8192,384]{2,1,0:T(8,128)(2,1)} %bitcast.18), custom_call_target="tpu_custom_call" | custom-call | tf_op jit(solution)/shard_map/pallas_call | solution.py:210
  25.1 2.9 %all-to-all-done = bf16[8,3,32,384]{3,2,1,0:T(8,128)(2,1)S(1)} async-done(((bf16[8,3,32,384]{3,2,1,0:T(8,128)(2,1)}), bf16[8,3,32,384]{3,2,1,0:T(8,128)(2,1)S(1)}, u32[]{:S(2)}, u32[]{:S(2)}) %all-to-all-start) | async-done | bytes 589856 | tf_op jit(solution)/shard_map/all_to_all | solution.py:228
  28.1 1.7 %collective-permute-start = (bf16[8,2,32,384]{3,2,1,0:T(8,128)(2,1)S(1)}, bf16[8,2,32,384]{3,2,1,0:T(8,128)(2,1)S(1)}, u32[]{:S(2)}, u32[]{:S(2)}) collective-permute-start(bf16[8,2,32,384]{3,2,1,0:T(8,128)(2,1)S(1)} %slice.7.own_ref), channel_id=1, source_target_pairs={{0,16},{8,24},{16,32},{24,40},{32,48},{40,56},{48,64},{56,72},{64,... | collective-permute-start | bytes 1179656 | tf_op jit(solution)/shard_map/ppermute | solution.py:224
  29.7 3.8 %collective-permute-start.1 = (bf16[8,2,32,384]{3,2,1,0:T(8,128)(2,1)S(1)}, bf16[8,2,32,384]{3,2,1,0:T(8,128)(2,1)S(1)}, u32[]{:S(2)}, u32[]{:S(2)}) collective-permute-start(bf16[8,2,32,384]{3,2,1,0:T(8,128)(2,1)S(1)} %slice.7.own_ref), channel_id=1, source_target_pairs={{0,240},{8,248},{16,0},{24,8},{32,16},{40,24},{48,32},{56,40},{64,... | collective-permute-start | bytes 1179656 | tf_op jit(solution)/shard_map/ppermute | solution.py:224
  33.5 0.0 collective-permute-start.2
  33.5 9.5 %shard_map.47 = (f32[3,256,128]{2,1,0:T(8,128)S(1)}, f32[3,256,128]{2,1,0:T(8,128)S(1)}, f32[3,256,128]{2,1,0:T(8,128)S(1)}) custom-call(s32[33]{0:T(128)S(1)} %get-tuple-element.25.order_ref, bf16[2,8192,384]{2,1,0:T(8,128)(2,1)} %bitcast.19, bf16[8,32,384]{2,1,0:T(8,128)(2,1)S(1)} %slice_bitcast_fusion.query_ref, ...), custom_call_target="tpu_custom_call" | custom-call | flops 4831838208 | bytes 9437184 | tf_op jit(solution)/shard_map/pallas_call | solution.py:196
  43.0 0.0 collective-permute-done.behind_ref
  43.0 0.0 collective-permute-done.1.ahead_ref
  43.0 0.1 broadcast_select_fusion
  43.1 2.1 %collective-permute-start.3 = (bf16[8,2,32,384]{3,2,1,0:T(8,128)(2,1)S(1)}, bf16[8,2,32,384]{3,2,1,0:T(8,128)(2,1)S(1)}, u32[]{:S(2)}, u32[]{:S(2)}) collective-permute-start(bf16[8,2,32,384]{3,2,1,0:T(8,128)(2,1)S(1)} %broadcast_select_fusion), channel_id=1, source_target_pairs={{0,248},{8,16},{16,8},{24,32},{32,24},{40,48},{48,40},{56,64},{64,... | collective-permute-start | bytes 1179656 | tf_op jit(solution)/shard_map/ppermute | solution.py:224
  45.2 0.0 collective-permute-start.4
  45.2 0.5 collective-permute-start.5
  45.7 0.0 collective-permute-done.2.beside_ref
  45.7 3.5 %shard_map.48 = (f32[3,256,128]{2,1,0:T(8,128)S(1)}, f32[3,256,128]{2,1,0:T(8,128)S(1)}, f32[3,256,128]{2,1,0:T(8,128)S(1)}) custom-call(s32[1]{0:T(128)} %bitcast.me_ref, s32[32]{0:T(128)S(1)} %copy-done, s32[1,6]{1,0:T(1,128)S(1)} %copy-done.1, s32[33]{0:T(128)S(1)} %get-tuple-element.25.order_ref, bf16[2,8192,384]{2,1,0:T(8,128)(2,1)} %bitcast.20, ...), custom_call_target="tpu_custom_call" | custom-call | flops 1610612736 | bytes 3145728 | tf_op jit(solution)/shard_map/pallas_call | solution.py:196
  49.2 4.5 %collective-permute-done.3.far_ref = bf16[8,2,32,384]{3,2,1,0:T(8,128)(2,1)S(1)} collective-permute-done((bf16[8,2,32,384]{3,2,1,0:T(8,128)(2,1)S(1)}, bf16[8,2,32,384]{3,2,1,0:T(8,128)(2,1)S(1)}, u32[]{:S(2)}, u32[]{:S(2)}) %collective-permute-start.3) | collective-permute-done | bytes 393248 | tf_op jit(solution)/shard_map/ppermute | solution.py:224
  53.7 0.0 collective-permute-done.4.beside_behind_ref
  53.7 0.0 collective-permute-done.5.beside_ahead_ref
  53.7 1.8 %shard_map.49 = bf16[8,32,384]{2,1,0:T(8,128)(2,1)S(1)} custom-call(s32[1]{0:T(128)} %bitcast.me_ref, s32[32]{0:T(128)S(1)} %copy-done, s32[1,6]{1,0:T(1,128)S(1)} %copy-done.1, bf16[8,32,384]{2,1,0:T(8,128)(2,1)S(1)} %slice_bitcast_fusion.query_ref, f32[3,256,128]{2,1,0:T(8,128)S(1)} %get-tuple-element.36.top_in, ...), custom_call_target="tpu_custom_call" | custom-call | flops 603979776 | bytes 1179648 | tf_op jit(solution)/shard_map/pallas_call | solution.py:196
  55.5 12.3 %all_to_all.10 = bf16[8,32,384]{2,1,0:T(8,128)(2,1)S(1)} all-to-all(bf16[8,32,384]{2,1,0:T(8,128)(2,1)S(1)} %shard_map.49), channel_id=1, replica_groups=mesh['pipe'=32,'uly'=8] {'uly'}, dimensions={0} | all-to-all | bytes 393216 | tf_op jit(solution)/shard_map/all_to_all | solution.py:228
  67.8 0.7 %copy.10 = bf16[8,4,8,384]{3,2,0,1:T(8,128)(2,1)} copy(bf16[8,4,8,384]{3,2,1,0:T(8,128)(2,1)S(1)} %bitcast.21) | data formatting | bytes 393216 | tf_op jit(solution)/shard_map/reshape | solution.py:261
  (2 shorter events, 0.1 us)
Async XLA Ops:
  2.0 26.0 %all-to-all-start = ((bf16[8,3,32,384]{3,2,1,0:T(8,128)(2,1)}), bf16[8,3,32,384]{3,2,1,0:T(8,128)(2,1)S(1)}, u32[]{:S(2)}, u32[]{:S(2)}) async-start(bf16[8,3,32,384]{3,2,1,0:T(8,128)(2,1)} %bitcast.17), calls=%async_computation | async-start | bytes 1179648 | tf_op jit(solution)/shard_map/all_to_all | solution.py:228
  10.6 11.7 %copy-start = (s32[32]{0:T(128)S(1)}, s32[32]{0:T(128)}, u32[]{:S(2)}) copy-start(s32[32]{0:T(128)} %plan_ref.5) | copy-start | bytes 388
  10.6 11.7 %copy-start.1 = (s32[1,6]{1,0:T(1,128)S(1)}, s32[1,6]{1,0:T(1,128)}, u32[]{:S(2)}) copy-start(s32[1,6]{1,0:T(1,128)} %refresh_ref.5) | copy-start | bytes 76
  28.1 15.0 %collective-permute-start = (bf16[8,2,32,384]{3,2,1,0:T(8,128)(2,1)S(1)}, bf16[8,2,32,384]{3,2,1,0:T(8,128)(2,1)S(1)}, u32[]{:S(2)}, u32[]{:S(2)}) collective-permute-start(bf16[8,2,32,384]{3,2,1,0:T(8,128)(2,1)S(1)} %slice.7.own_ref), channel_id=1, source_target_pairs={{0,16},{8,24},{16,32},{24,40},{32,48},{40,56},{48,64},{56,72},{64,... | collective-permute-start | bytes 1179656 | tf_op jit(solution)/shard_map/ppermute | solution.py:224
  29.7 13.3 %collective-permute-start.1 = (bf16[8,2,32,384]{3,2,1,0:T(8,128)(2,1)S(1)}, bf16[8,2,32,384]{3,2,1,0:T(8,128)(2,1)S(1)}, u32[]{:S(2)}, u32[]{:S(2)}) collective-permute-start(bf16[8,2,32,384]{3,2,1,0:T(8,128)(2,1)S(1)} %slice.7.own_ref), channel_id=1, source_target_pairs={{0,240},{8,248},{16,0},{24,8},{32,16},{40,24},{48,32},{56,40},{64,... | collective-permute-start | bytes 1179656 | tf_op jit(solution)/shard_map/ppermute | solution.py:224
  33.5 12.2 %collective-permute-start.2 = (bf16[8,2,32,384]{3,2,1,0:T(8,128)(2,1)S(1)}, bf16[8,2,32,384]{3,2,1,0:T(8,128)(2,1)S(1)}, u32[]{:S(2)}, u32[]{:S(2)}) collective-permute-start(bf16[8,2,32,384]{3,2,1,0:T(8,128)(2,1)S(1)} %slice.7.own_ref), channel_id=1, source_target_pairs={{0,8},{8,0},{16,24},{24,16},{32,40},{40,32},{48,56},{56,48},{64,72... | collective-permute-start | bytes 1179656 | tf_op jit(solution)/shard_map/ppermute | solution.py:224
  43.1 10.6 %collective-permute-start.3 = (bf16[8,2,32,384]{3,2,1,0:T(8,128)(2,1)S(1)}, bf16[8,2,32,384]{3,2,1,0:T(8,128)(2,1)S(1)}, u32[]{:S(2)}, u32[]{:S(2)}) collective-permute-start(bf16[8,2,32,384]{3,2,1,0:T(8,128)(2,1)S(1)} %broadcast_select_fusion), channel_id=1, source_target_pairs={{0,248},{8,16},{16,8},{24,32},{32,24},{40,48},{48,40},{56,64},{64,... | collective-permute-start | bytes 1179656 | tf_op jit(solution)/shard_map/ppermute | solution.py:224
  45.2 8.5 %collective-permute-start.4 = (bf16[8,2,32,384]{3,2,1,0:T(8,128)(2,1)S(1)}, bf16[8,2,32,384]{3,2,1,0:T(8,128)(2,1)S(1)}, u32[]{:S(2)}, u32[]{:S(2)}) collective-permute-start(bf16[8,2,32,384]{3,2,1,0:T(8,128)(2,1)S(1)} %collective-permute-done.behind_ref), channel_id=1, source_target_pairs={{0,8},{8,0},{16,24},{24,16},{32,40},{40,32},{48,56},{56,48},{64,72... | collective-permute-start | bytes 1179656 | tf_op jit(solution)/shard_map/ppermute | solution.py:224
  45.2 8.5 %collective-permute-start.5 = (bf16[8,2,32,384]{3,2,1,0:T(8,128)(2,1)S(1)}, bf16[8,2,32,384]{3,2,1,0:T(8,128)(2,1)S(1)}, u32[]{:S(2)}, u32[]{:S(2)}) collective-permute-start(bf16[8,2,32,384]{3,2,1,0:T(8,128)(2,1)S(1)} %collective-permute-done.1.ahead_ref), channel_id=1, source_target_pairs={{0,8},{8,0},{16,24},{24,16},{32,40},{40,32},{48,56},{56,48},{64,72... | collective-permute-start | bytes 1179656 | tf_op jit(solution)/shard_map/ppermute | solution.py:224
